TPU v7x, 128 devices: a whole 4x4x4 slice. The times are simulated.
128 devices in a mesh: row: 32 (over z, y, x_hi), col: 4 (over x_lo, core).
Axes of the slice: x: 4 (x_hi: 2, x_lo: 2; x = x_hi * 2 + x_lo), y: 4, z: 4, core: 2. Of those that a mesh axis runs over, the one named last changes fastest.
Arguments:
- rhs_child: float32 [256, 131072], P(None, ('row', 'col')), may hold values from -8 to 8
- rhs_parent: float32 [256, 131072], P('col', 'row'), may hold values from -8 to 8
- dinv_child: bfloat16 [131072, 4096], P('row', 'col'), may hold values from -0.09375 to 0.09375
- dinv_parent: bfloat16 [131072, 4096], P('row', 'col'), may hold values from -0.09375 to 0.09375
- ubase_child: bfloat16 [64, 131072], P(None, ('row', 'col')), may hold values from -0.09375 to 0.09375
- vbase_child: bfloat16 [64, 131072], P(None, ('row', 'col')), may hold values from -0.09375 to 0.09375
- ubase_parent: bfloat16 [64, 131072], P(None, ('row', 'col')), may hold values from -0.09375 to 0.09375
- vbase_parent: bfloat16 [64, 131072], P(None, ('row', 'col')), may hold values from -0.09375 to 0.09375
- trans_child: float32 [32, 64, 64], P('row'), may hold values from -1 to 2
- trans_parent: float32 [32, 64, 64], P('row'), may hold values from -1 to 2
- w_first: bfloat16 [64, 131072], P(None, ('row', 'col')), may hold values from -0.5 to 0.5
- w_second: bfloat16 [32, 262144], P(None, 'row'), may hold values from -1 to 1
- block_ranks: int32 [1024], P(('row', 'col')), may hold values from 16 to 64
- extend_map: int32 [2048], replicated, may hold values from 0 to 1023, as said below
Outputs:
- x_child: float32 [256, 131072], P(None, ('row', 'col'))
- x_parent: float32 [256, 131072], P(None, ('row', 'col'))
Inputs may be any that keep to these rules, and one draw needn't show every extreme that they name: `extend_map`: entries i * 64 to i * 64 + 63 belong to row index i. The entries of the first half of the row indices name every parent block exactly once, and so do those of the second half. Parent block p is held by row index p // 32. From one row index, 0, half of 4, or 4 entries name blocks held by one row index, and every row index sends 4 to some row index.
All inputs are finite; a program needn't handle non-finite values.
Results may differ from a plain program's by a relative error of at most 0.028.
Values may be sent and summed in bfloat16 or wider, within the bound.
A program may use at most 128 MiB of HBM per device.

v0:
```python
import jax
import jax.numpy as jnp
from jax import lax
from jax.sharding import PartitionSpec as P

PRECISE = lax.Precision.HIGHEST


def prefix_2(part, axis, combine, identity, reverse):
    count = lax.axis_size(axis)
    place = lax.axis_index(axis)
    ahead = count - 1 - place if reverse else place
    gathered = jax.tree.map(lambda a: lax.all_gather(a, axis), part)
    state = jax.tree.map(lambda a, e: jnp.zeros_like(a) + jnp.asarray(e, a.dtype), part, identity)

    def one(hop, state):
        source = count - 1 - hop if reverse else hop
        return combine(
            state, jax.tree.map(lambda a: lax.dynamic_index_in_dim(a, source, 0, False), gathered)
        )

    return lax.fori_loop(0, ahead, one, state)


def column_swap(pieces):
    return lax.all_to_all(pieces, "col", split_axis=0, concat_axis=1, tiled=True)


def extend_swap(bucket_contents):
    return lax.all_to_all(bucket_contents, "row", split_axis=0, concat_axis=0, tiled=True)


def column_sums(first_term, second_term):
    return (
        lax.psum(first_term.astype(jnp.bfloat16), "col").astype(jnp.float32),
        lax.psum(second_term.astype(jnp.bfloat16), "col").astype(jnp.float32),
    )


def gather_apply(matrix, stacked):
    return lax.dot_general(
        matrix,
        lax.all_gather(stacked, "col", axis=1, tiled=True),
        (((0,), (1,)), ((), ())),
        preferred_element_type=jnp.float32,
    )


def sum_apply(matrix, stacked):
    return lax.psum_scatter(
        lax.dot_general(
            matrix, stacked, (((1,), (1,)), ((), ())), preferred_element_type=jnp.float32
        ).astype(jnp.bfloat16),
        "col",
        scatter_dimension=0,
        tiled=True,
    ).astype(jnp.float32)


def compose(before_pair, after_pair):
    joined = jnp.dot(after_pair[0], before_pair[0], precision=PRECISE)
    shifted = jnp.dot(after_pair[0], before_pair[1], precision=PRECISE) + after_pair[1]
    return (joined, shifted)


def chain_states(transfer, source, series_extent, backward):
    position = lax.axis_index("row")
    boundary = (
        position % series_extent == 0 if backward else position % series_extent == series_extent - 1
    )
    retain = jnp.where(boundary, 0.0, 1.0).astype(jnp.float32)
    transfer = transfer * retain
    source = source * retain
    identity = (jnp.eye(transfer.shape[0], dtype=jnp.float32), jnp.zeros_like(source))
    prefix = prefix_2((transfer, source), "row", compose, identity, backward)
    result_states = prefix[1]
    return result_states


def lower_solve(inverse, left_base, right_base, transfer, rhs_block, series_extent):
    rhs_count = rhs_block.shape[0]
    stacked = jnp.concatenate([rhs_block, left_base], axis=0)
    product = sum_apply(inverse, stacked)
    direct = product[:, :rhs_count]
    coupled = product[:, rhs_count:]
    vfloat = right_base.astype(jnp.float32)
    source, kernel = column_sums(
        jnp.dot(vfloat, direct, precision=PRECISE), jnp.dot(vfloat, coupled, precision=PRECISE)
    )
    states = chain_states(transfer[0] - kernel, source, series_extent, False)
    return (direct - jnp.dot(coupled, states, precision=PRECISE)).T


def upper_solve(inverse, left_base, right_base, transfer, rhs_block, series_extent):
    rhs_count = rhs_block.shape[0]
    stacked = jnp.concatenate([rhs_block, right_base], axis=0)
    product = gather_apply(inverse, stacked)
    direct = product[:, :rhs_count]
    coupled = product[:, rhs_count:]
    ufloat = left_base.astype(jnp.float32)
    source, kernel = column_sums(
        jnp.dot(ufloat, direct, precision=PRECISE), jnp.dot(ufloat, coupled, precision=PRECISE)
    )
    states = chain_states(transfer[0].T - kernel, source, series_extent, True)
    return (direct - jnp.dot(coupled, states, precision=PRECISE)).T


def shards(
    rhs_child,
    rhs_parent,
    dinv_child,
    dinv_parent,
    ubase_child,
    vbase_child,
    ubase_parent,
    vbase_parent,
    trans_child,
    trans_parent,
    w_first,
    w_second,
    block_ranks,
    extend_map,
):
    row_count = lax.axis_size("row")
    col_count = lax.axis_size("col")
    position = lax.axis_index("row")
    half_chain = row_count // 2
    y_child = lower_solve(
        dinv_child,
        ubase_child,
        vbase_child,
        trans_child,
        rhs_child.astype(jnp.bfloat16),
        half_chain,
    )
    y_round = y_child.astype(jnp.bfloat16)
    rhs_count, local_rows = y_child.shape
    rank_pad = w_first.shape[0]
    group_count = block_ranks.shape[0]
    block_rows = local_rows // group_count
    rhs_share = rhs_count // col_count
    allowed = (jnp.arange(rank_pad, dtype=jnp.int32)[:, None] < block_ranks[None, :]).astype(
        jnp.bfloat16
    )
    masked = w_first.reshape(rank_pad, group_count, block_rows) * allowed[:, :, None]
    shaped = y_round.reshape(col_count, rhs_share, group_count, block_rows)
    factor = jnp.einsum(
        "rga,pkga->pgkr", masked, shaped, preferred_element_type=jnp.float32
    ).astype(jnp.bfloat16)
    arrived = column_swap(factor.reshape(col_count, group_count, rhs_share * rank_pad))
    groups_all = arrived.shape[1]
    arrived = arrived.reshape(groups_all, rhs_share, rank_pad)
    second = w_second.reshape(groups_all, rank_pad, block_rows)
    slot_width = rhs_share * block_rows
    update = jnp.einsum("gbw,gsb->bsw", second, arrived, preferred_element_type=jnp.float32).astype(
        jnp.bfloat16
    )
    update = update.reshape(rank_pad, slot_width)
    parent_blocks = rhs_parent.shape[1] // block_rows
    capacity = 2 * rank_pad // row_count
    slot_count = row_count * capacity
    target = (extend_map // parent_blocks).reshape(row_count, rank_pad)
    placed = (extend_map % parent_blocks).reshape(row_count, rank_pad)
    serial = jnp.arange(rank_pad, dtype=jnp.int32)
    shared_destination = target[:, :, None] == target[:, None, :]
    before_mask = serial[None, :] < serial[:, None]
    earlier_count = jnp.sum(shared_destination & before_mask[None, :, :], axis=2, dtype=jnp.int32)
    my_slot = target[position] * capacity + earlier_count[position]
    send_hot = (jnp.arange(slot_count, dtype=jnp.int32)[:, None] == my_slot[None, :]).astype(
        jnp.bfloat16
    )
    arriving = target == position
    matches = (
        (
            placed[None, :, None, :]
            == jnp.arange(parent_blocks, dtype=jnp.int32)[:, None, None, None]
        )
        & (
            earlier_count[None, :, None, :]
            == jnp.arange(capacity, dtype=jnp.int32)[None, None, :, None]
        )
        & arriving[None, :, None, :]
    )
    receive_onehot = (
        jnp.sum(matches, axis=3, dtype=jnp.int32)
        .reshape(parent_blocks, slot_count)
        .astype(jnp.bfloat16)
    )
    outgoing = jnp.dot(send_hot, update, preferred_element_type=jnp.float32).astype(jnp.bfloat16)
    incoming = extend_swap(outgoing.reshape(row_count, capacity, slot_width))
    contrib = jnp.dot(
        receive_onehot, incoming.reshape(slot_count, slot_width), preferred_element_type=jnp.float32
    )
    contrib = (
        contrib.reshape(parent_blocks, rhs_share, block_rows)
        .transpose(1, 0, 2)
        .reshape(rhs_share, parent_blocks * block_rows)
    )
    rhs_split = (rhs_parent - contrib).astype(jnp.bfloat16)
    rhs_split = rhs_split.reshape(rhs_share, col_count, local_rows).transpose(1, 0, 2)
    parent_rhs = column_swap(rhs_split).reshape(rhs_count, local_rows)
    y_parent = lower_solve(
        dinv_parent, ubase_parent, vbase_parent, trans_parent, parent_rhs, row_count
    )
    x_parent = upper_solve(
        dinv_parent,
        ubase_parent,
        vbase_parent,
        trans_parent,
        y_parent.astype(jnp.bfloat16),
        row_count,
    )
    x_round = x_parent.astype(jnp.bfloat16)
    returned = column_swap(x_round.reshape(col_count, rhs_share, local_rows)).reshape(
        col_count, rhs_share, local_rows
    )
    x_blocks = (
        returned.transpose(1, 0, 2)
        .reshape(rhs_share, parent_blocks, block_rows)
        .transpose(1, 0, 2)
        .reshape(parent_blocks, slot_width)
    )
    replies = lax.dot_general(
        receive_onehot, x_blocks, (((0,), (0,)), ((), ())), preferred_element_type=jnp.float32
    ).astype(jnp.bfloat16)
    answers = extend_swap(replies.reshape(row_count, capacity, slot_width))
    picked = lax.dot_general(
        send_hot,
        answers.reshape(slot_count, slot_width),
        (((0,), (0,)), ((), ())),
        preferred_element_type=jnp.float32,
    ).astype(jnp.bfloat16)
    picked = picked.reshape(rank_pad, rhs_share, block_rows)
    pulled = jnp.einsum("gbw,bsw->gsb", second, picked, preferred_element_type=jnp.float32).astype(
        jnp.bfloat16
    )
    returned_factor = column_swap(pulled.reshape(col_count, group_count, rhs_share * rank_pad))
    returned_factor = returned_factor.reshape(col_count, group_count, rhs_share, rank_pad)
    correction = jnp.einsum(
        "rga,pgkr->pkga", masked, returned_factor, preferred_element_type=jnp.float32
    ).reshape(rhs_count, local_rows)
    child_z = (y_child - correction).astype(jnp.bfloat16)
    x_child = upper_solve(dinv_child, ubase_child, vbase_child, trans_child, child_z, half_chain)
    return (x_child, x_parent)


def solution(mesh):
    return jax.shard_map(
        shards,
        mesh=mesh,
        in_specs=(
            P(None, ("row", "col")),
            P("col", "row"),
            P("row", "col"),
            P("row", "col"),
            P(None, ("row", "col")),
            P(None, ("row", "col")),
            P(None, ("row", "col")),
            P(None, ("row", "col")),
            P("row", None, None),
            P("row", None, None),
            P(None, ("row", "col")),
            P(None, "row"),
            P(("row", "col")),
            P(),
        ),
        out_specs=(P(None, ("row", "col")), P(None, ("row", "col"))),
        check_vma=False,
    )
```

profile of v0, /device:TPU:1, one launch (start us, length us, event | category | flops | bytes accessed | tf_op | source)
XLA Modules:
  0.0 925.5 jit_solution(792028130411712138)
XLA Ops:
  8.6 7.9 fusion.12
  16.6 36.0 %reduce-scatter.3.cloned.1.call-done = bf16[1024,320]{0,1:T(8,128)(2,1)} async-done(((bf16[4096,320]{0,1:T(8,128)(2,1)}), bf16[1024,320]{0,1:T(8,128)(2,1)}) %reduce-scatter.3.cloned.1.call-update) | async-done | bytes 655376 | tf_op jit(solution)/shard_map/reduce_scatter | solution.py:50
  55.0 10.6 %all-reduce.3 = (bf16[64,64]{0,1:T(8,128)(2,1)S(1)}, bf16[64,256]{1,0:T(8,128)(2,1)S(1)}) all-reduce(bf16[64,64]{0,1:T(8,128)(2,1)S(1)} %fusion.26, bf16[64,256]{1,0:T(8,128)(2,1)S(1)} %fusion.22), channel_id=1, replica_groups=mesh['row'=32,'col'=4] {'col'}, use_global_device_ids=true, to_apply=%region_1.0 | all-reduce | flops 20480 | bytes 81920 | tf_op jit(solution)/shard_map/psum | solution.py:36
  66.6 91.4 %all-gather = f32[2048,64]{1,0:T(8,128)S(1)} all-gather(f32[64,64]{1,0:T(8,128)S(1)} %copy.92), channel_id=2, replica_groups=mesh['row'=32,'col'=4] {'row'}, dimensions={0}, use_global_device_ids=true | all-gather | bytes 540672 | tf_op jit(solution)/shard_map/all_gather | solution.py:13
  161.7 18.7 %all-to-all-start = ((bf16[4,8,4096]{2,1,0:T(8,128)(2,1)}), bf16[4,8,4096]{2,1,0:T(8,128)(2,1)S(1)}, u32[]{:S(2)}, u32[]{:S(2)}) async-start(bf16[4,8,4096]{2,1,0:T(8,128)(2,1)} %copy.96), calls=%async_computation.1 | async-start | bytes 524288 | tf_op jit(solution)/shard_map/all_to_all | solution.py:26
  193.5 35.4 %all-to-all-start.1 = ((bf16[32,4,8192]{2,1,0:T(4,128)(2,1)}), bf16[32,4,8192]{2,1,0:T(4,128)(2,1)}, u32[]{:S(2)}, u32[]{:S(2)}) async-start(bf16[32,4,8192]{2,1,0:T(4,128)(2,1)} %reshape.159), calls=%async_computation.2 | async-start | bytes 4194304 | tf_op jit(solution)/shard_map/all_to_all | solution.py:30
  231.8 26.2 %all-to-all-done.1 = bf16[32,4,8192]{2,1,0:T(4,128)(2,1)} async-done(((bf16[32,4,8192]{2,1,0:T(4,128)(2,1)}), bf16[32,4,8192]{2,1,0:T(4,128)(2,1)}, u32[]{:S(2)}, u32[]{:S(2)}) %all-to-all-start.1) | async-done | bytes 2097184 | tf_op jit(solution)/shard_map/all_to_all | solution.py:30
  269.7 12.7 %all_to_all.46 = bf16[4,64,1024]{2,1,0:T(8,128)(2,1)S(1)} all-to-all(bf16[4,64,1024]{2,1,0:T(8,128)(2,1)S(1)} %copy.101), channel_id=1, replica_groups=mesh['row'=32,'col'=4] {'col'}, dimensions={0} | all-to-all | bytes 1048576 | tf_op jit(solution)/shard_map/all_to_all | solution.py:26
  282.4 10.3 %fusion.13 = bf16[4096,320]{0,1:T(8,128)(2,1)} fusion(bf16[4096,1024]{1,0:T(8,128)(2,1)} %param.25, bf16[64,1024]{1,0:T(8,128)(2,1)S(1)} %copy-done.2, bf16[256,1024]{1,0:T(8,128)(2,1)S(1)} %bitcast.230), kind=kOutput, calls=%fused_computation.22 | convolution fusion | flops 2686976000 | bytes 11665408 | tf_op jit(solution)/shard_map/dot_general | solution.py:51
  292.8 29.1 %reduce-scatter.5.cloned.1.call-done = bf16[1024,320]{0,1:T(8,128)(2,1)} async-done(((bf16[4096,320]{0,1:T(8,128)(2,1)}), bf16[1024,320]{0,1:T(8,128)(2,1)}) %reduce-scatter.5.cloned.1.call-update) | async-done | bytes 655376 | tf_op jit(solution)/shard_map/reduce_scatter | solution.py:50
  324.3 10.6 %all-reduce.2 = (bf16[64,64]{0,1:T(8,128)(2,1)S(1)}, bf16[64,256]{1,0:T(8,128)(2,1)S(1)}) all-reduce(bf16[64,64]{0,1:T(8,128)(2,1)S(1)} %fusion.27, bf16[64,256]{1,0:T(8,128)(2,1)S(1)} %fusion.23), channel_id=1, replica_groups=mesh['row'=32,'col'=4] {'col'}, use_global_device_ids=true, to_apply=%region_8.9 | all-reduce | flops 20480 | bytes 81920 | tf_op jit(solution)/shard_map/psum | solution.py:36
  335.8 91.7 %all-gather.2 = f32[2048,64]{1,0:T(8,128)S(1)} all-gather(f32[64,64]{1,0:T(8,128)S(1)} %copy.103), channel_id=4, replica_groups=mesh['row'=32,'col'=4] {'row'}, dimensions={0}, use_global_device_ids=true | all-gather | bytes 540672 | tf_op jit(solution)/shard_map/all_gather | solution.py:13
  430.2 76.2 %all-gather.15.cloned.1.call-done = bf16[320,4096]{1,0:T(8,128)(2,1)} async-done(((bf16[320,1024]{1,0:T(8,128)(2,1)}), bf16[320,4096]{1,0:T(8,128)(2,1)}) %all-gather.15.cloned.1.call-update) | async-done | bytes 2621456 | tf_op jit(solution)/shard_map/all_gather | solution.py:43
  506.4 6.1 convolution_bitcast_fusion.1
  513.5 10.6 %all-reduce.1 = (bf16[64,64]{1,0:T(8,128)(2,1)S(1)}, bf16[64,256]{1,0:T(8,128)(2,1)S(1)}) all-reduce(bf16[64,64]{1,0:T(8,128)(2,1)S(1)} %fusion.28, bf16[64,256]{1,0:T(8,128)(2,1)S(1)} %fusion.24), channel_id=1, replica_groups=mesh['row'=32,'col'=4] {'col'}, use_global_device_ids=true, to_apply=%region_12.13 | all-reduce | flops 20480 | bytes 81920 | tf_op jit(solution)/shard_map/psum | solution.py:36
  524.8 96.0 %all-gather.4 = f32[2048,64]{1,0:T(8,128)} all-gather(f32[64,64]{1,0:T(8,128)S(1)} %fusion.65), channel_id=6, replica_groups=mesh['row'=32,'col'=4] {'row'}, dimensions={0}, use_global_device_ids=true | all-gather | bytes 540672 | tf_op jit(solution)/shard_map/all_gather | solution.py:13
  620.9 34.2 %while.54 = (s32[]{:T(128)}, f32[64,256]{1,0:T(8,128)S(1)}, s32[]{:T(128)}, f32[32,64,64]{2,1,0:T(8,128)}, f32[32,64,256]{2,1,0:T(8,128)}, /*index=5*/s32[]{:T(128)}, s32[]{:T(128)}, s32[]{:T(128)}, s32[]{:T(128)}) while((s32[]{:T(128)}, f32[64,256]{1,0:T(8,128)S(1)}, s32[]{:T(128)}, f32[32,64,64]{2,1,0:T(8,128)}, ...), condition=%wide.region_15.16_spmd, body=%wide.region_14.15_spmd.sunk | while | flops 12599302 | bytes 361611 | solution.py:22
  657.1 25.0 %all_to_all.47 = bf16[4,64,1024]{2,1,0:T(8,128)(2,1)S(1)} all-to-all(bf16[4,64,1024]{2,1,0:T(8,128)(2,1)S(1)} %bitcast.224), channel_id=1, replica_groups=mesh['row'=32,'col'=4] {'col'}, dimensions={0} | all-to-all | bytes 1048576 | tf_op jit(solution)/shard_map/all_to_all | solution.py:26
  688.7 34.0 %all_to_all.48 = bf16[32,4,8192]{2,1,0:T(4,128)(2,1)} all-to-all(bf16[32,4,8192]{2,1,0:T(4,128)(2,1)} %reshape.167), channel_id=1, replica_groups=mesh['row'=32,'col'=4] {'row'}, dimensions={0} | all-to-all | bytes 4194304 | tf_op jit(solution)/shard_map/all_to_all | solution.py:30
  730.8 9.6 %all_to_all.49 = bf16[4,8,4096]{2,1,0:T(8,128)(2,1)S(1)} all-to-all(bf16[4,8,4096]{2,1,0:T(8,128)(2,1)S(1)} %reshape.170), channel_id=1, replica_groups=mesh['row'=32,'col'=4] {'col'}, dimensions={0} | all-to-all | bytes 524288 | tf_op jit(solution)/shard_map/all_to_all | solution.py:26
  743.4 29.7 %all-gather.17.cloned.1.call-done = bf16[320,4096]{1,0:T(8,128)(2,1)} async-done(((bf16[320,1024]{1,0:T(8,128)(2,1)}), bf16[320,4096]{1,0:T(8,128)(2,1)}) %all-gather.17.cloned.1.call-update) | async-done | bytes 2621456 | tf_op jit(solution)/shard_map/all_gather | solution.py:43
  780.2 10.6 %all-reduce = (bf16[64,64]{1,0:T(8,128)(2,1)S(1)}, bf16[64,256]{1,0:T(8,128)(2,1)S(1)}) all-reduce(bf16[64,64]{1,0:T(8,128)(2,1)S(1)} %fusion.29, bf16[64,256]{1,0:T(8,128)(2,1)S(1)} %fusion.25), channel_id=1, replica_groups=mesh['row'=32,'col'=4] {'col'}, use_global_device_ids=true, to_apply=%region_16.17 | all-reduce | flops 20480 | bytes 81920 | tf_op jit(solution)/shard_map/psum | solution.py:36
  791.5 91.6 %all-gather.6 = f32[2048,64]{1,0:T(8,128)S(1)} all-gather(f32[64,64]{1,0:T(8,128)S(1)} %fusion.64), channel_id=8, replica_groups=mesh['row'=32,'col'=4] {'row'}, dimensions={0}, use_global_device_ids=true | all-gather | bytes 540672 | tf_op jit(solution)/shard_map/all_gather | solution.py:13
  883.1 33.6 %while.55 = (s32[]{:T(128)}, f32[64,256]{1,0:T(8,128)S(1)}, s32[]{:T(128)}, f32[32,64,64]{2,1,0:T(8,128)S(1)}, f32[32,64,256]{2,1,0:T(8,128)}, /*index=5*/s32[]{:T(128)}, s32[]{:T(128)}, s32[]{:T(128)}, s32[]{:T(128)}) while((s32[]{:T(128)}, f32[64,256]{1,0:T(8,128)S(1)}, s32[]{:T(128)}, f32[32,64,64]{2,1,0:T(8,128)S(1)}, ...), condition=%wide.region_19.20_spmd, body=%wide.region_18.19_spmd.sunk | while | flops 12599302 | bytes 361611 | solution.py:22
  (245 shorter events, 138.4 us)
Async XLA Ops:
  7.2 179.6 %copy-start = (bf16[32,8192]{1,0:T(8,128)(2,1)S(1)}, bf16[32,8192]{1,0:T(8,128)(2,1)}, u32[]{:S(2)}) copy-start(bf16[32,8192]{1,0:T(8,128)(2,1)} %param.33) | copy-start | bytes 1572868
  7.2 45.4 %reduce-scatter.3.cloned.1.call-start = ((), (), s32[]{:S(2)}) async-start(), calls=%async_computation.8 | async-start | bytes 3276800 | tf_op jit(solution)/shard_map/reduce_scatter | solution.py:50
  16.5 36.1 %copy-start.5 = (bf16[64,1024]{1,0:T(8,128)(2,1)S(1)}, bf16[64,1024]{1,0:T(8,128)(2,1)}, u32[]{:S(2)}) copy-start(bf16[64,1024]{1,0:T(8,128)(2,1)} %param.27) | copy-start | bytes 393220
  16.5 49.8 %copy-start.7 = (f32[1,64,64]{2,1,0:T(8,128)S(1)}, f32[1,64,64]{2,1,0:T(8,128)}, u32[]{:S(2)}) copy-start(f32[1,64,64]{2,1,0:T(8,128)} %param.30) | copy-start | bytes 49156
  16.5 49.9 %copy-start.9 = (s32[2048]{0:T(1024)S(1)}, s32[2048]{0:T(1024)}, u32[]{:S(2)}) copy-start(s32[2048]{0:T(1024)} %param.35) | copy-start | bytes 24580
  16.5 50.0 %copy-start.10 = (s32[8]{0:T(128)S(1)}, s32[8]{0:T(128)}, u32[]{:S(2)}) copy-start(s32[8]{0:T(128)} %param.34) | copy-start | bytes 100
  16.5 141.5 %all-gather.19.cloned.1.call-start = ((), (), s32[]{:S(2)}) async-start(), calls=%async_computation.12 | async-start | bytes 2162688 | tf_op jit(solution)/shard_map/all_gather | solution.py:13
  158.1 2.0 copy-start.6
  161.7 23.7 %all-to-all-start = ((bf16[4,8,4096]{2,1,0:T(8,128)(2,1)}), bf16[4,8,4096]{2,1,0:T(8,128)(2,1)S(1)}, u32[]{:S(2)}, u32[]{:S(2)}) async-start(bf16[4,8,4096]{2,1,0:T(8,128)(2,1)} %copy.96), calls=%async_computation.1 | async-start | bytes 524288 | tf_op jit(solution)/shard_map/all_to_all | solution.py:26
  193.5 64.4 %all-to-all-start.1 = ((bf16[32,4,8192]{2,1,0:T(4,128)(2,1)}), bf16[32,4,8192]{2,1,0:T(4,128)(2,1)}, u32[]{:S(2)}, u32[]{:S(2)}) async-start(bf16[32,4,8192]{2,1,0:T(4,128)(2,1)} %reshape.159), calls=%async_computation.2 | async-start | bytes 4194304 | tf_op jit(solution)/shard_map/all_to_all | solution.py:30
  228.9 92.9 %reduce-scatter.5.cloned.1.call-start = ((), (), s32[]{:S(2)}) async-start(), calls=%async_computation.9 | async-start | bytes 3276800 | tf_op jit(solution)/shard_map/reduce_scatter | solution.py:50
  266.0 2.5 copy-start.1
  269.2 13.2 %copy-start.2 = (bf16[64,1024]{1,0:T(8,128)(2,1)S(1)}, bf16[64,1024]{1,0:T(8,128)(2,1)}, u32[]{:S(2)}) copy-start(bf16[64,1024]{1,0:T(8,128)(2,1)} %param.28) | copy-start | bytes 393220
  292.7 29.2 %copy-start.4 = (bf16[64,1024]{1,0:T(8,128)(2,1)S(1)}, bf16[64,1024]{1,0:T(8,128)(2,1)}, u32[]{:S(2)}) copy-start(bf16[64,1024]{1,0:T(8,128)(2,1)} %param.29) | copy-start | bytes 393220
  292.7 42.9 %copy-start.8 = (f32[1,64,64]{2,1,0:T(8,128)S(1)}, f32[1,64,64]{2,1,0:T(8,128)}, u32[]{:S(2)}) copy-start(f32[1,64,64]{2,1,0:T(8,128)} %param.31) | copy-start | bytes 49156
  292.7 134.7 %all-gather.21.cloned.1.call-start = ((), (), s32[]{:S(2)}) async-start(), calls=%async_computation.13 | async-start | bytes 2162688 | tf_op jit(solution)/shard_map/all_gather | solution.py:13
  335.5 170.9 %all-gather.15.cloned.1.call-start = ((), (), s32[]{:S(2)}) async-start(), calls=%async_computation.10 | async-start | bytes 3276800 | tf_op jit(solution)/shard_map/all_gather | solution.py:43
  430.1 190.7 %all-gather.23.cloned.1.call-start = ((), (), s32[]{:S(2)}) async-start(), calls=%async_computation.14 | async-start | bytes 2162688 | tf_op jit(solution)/shard_map/all_gather | solution.py:13
  524.7 248.4 %all-gather.17.cloned.1.call-start = ((), (), s32[]{:S(2)}) async-start(), calls=%async_computation.11 | async-start | bytes 3276800 | tf_op jit(solution)/shard_map/all_gather | solution.py:43
  743.3 139.7 %all-gather.25.cloned.1.call-start = ((), (), s32[]{:S(2)}) async-start(), calls=%async_computation.15 | async-start | bytes 2162688 | tf_op jit(solution)/shard_map/all_gather | solution.py:13
  743.4 35.8 %copy-start.3 = (bf16[64,1024]{1,0:T(8,128)(2,1)S(1)}, bf16[64,1024]{1,0:T(8,128)(2,1)}, u32[]{:S(2)}) copy-start(bf16[64,1024]{1,0:T(8,128)(2,1)} %param.26) | copy-start | bytes 393220
Sparse Core Ops, SparseCore 0:
  16.6 35.9 reduce-scatter.2
  66.4 73.5 all-gather.18
  292.8 28.9 reduce-scatter.4
  335.6 73.6 all-gather.20
  430.3 76.1 all-gather.14
  524.9 72.4 all-gather.22
  743.5 29.6 all-gather.16
  791.6 73.8 all-gather.24
where the time goes:
time: 944 us; the launch traced here: 926 us
  blocking collectives  494 us (52%)
  waiting for transfers between devices  202 us (21%)
  matrix products  120 us (13%)
  starting transfers between devices  54.6 us (6%)
  local copies, waits for them, and re-layouts  27.6 us (3%)
  between operations  14.7 us (2%)
  other arithmetic  10.2 us (1%)
    all_gather x4, blocking collectives, prefix_2(): gathered = jax.tree.map(lambda a: lax.all_gather(a, axis), part)  371 us
    all_gather x2, waiting for transfers between devices, gather_apply(): lax.all_gather(stacked, 'col', axis=1, tiled=True)  106 us
    reduce_scatter x2, waiting for transfers between devices, sum_apply(): lax.psum_scatter(lax.dot_general(matrix, stacked, (((1,), (1,)), ((), ())...  65.1 us
    dot_general x62, matrix products, compose(): jnp.dot(after_pair[0], before_pair[1], precision=PRECISE) + after_pair[1]  65 us
    all_to_all x3, blocking collectives, column_swap(): lax.all_to_all(pieces, 'col', split_axis=0, concat_axis=1, tiled=True)  47.3 us
    psum x4, blocking collectives, column_sums(): lax.psum(second_term.astype(jnp.bfloat16), 'col').astype(jnp.float32)  42.3 us
    all_to_all x1, starting transfers between devices, extend_swap(): lax.all_to_all(bucket_contents, 'row', split_axis=0, concat_axis=0, tiled...  35.4 us
    all_to_all x1, blocking collectives, extend_swap(): lax.all_to_all(bucket_contents, 'row', split_axis=0, concat_axis=0, tiled...  34 us
  transfers between devices with their start and end apart: 10, of which 6 were waited for; matrix products, arithmetic and copies ran while one was open for 0% of the time, Pallas kernels for 0%

commit v1 on v0

v1 whole, which is shorter than its diff:
```python
from typing import Any, NamedTuple

import jax
import jax.numpy as jnp
from jax import lax
from jax.experimental import pallas as pl
from jax.experimental.pallas import tpu as pltpu
from jax.sharding import PartitionSpec as P

MESH = pl.DeviceIdType.MESH
F32 = jnp.float32
BF16 = jnp.bfloat16
HIGH = lax.Precision.HIGHEST

ROWS = 32
COLS = 4
HALF = 16
H = 256
HS = 64
RANK = 64
NLOC = 1024
GROUPS = 8
BLK = 128
SUBS = 4
SUB = NLOC // SUBS
SLOTS = 4

DMA = pltpu.SemaphoreType.DMA


class Link(NamedTuple):
    src: Any
    dst: Any
    sent: Any
    came: Any


class Hops(NamedTuple):
    buf: Any
    sent: Any
    came: Any


class Sums(NamedTuple):
    a: Link
    b: Link
    acc: Any


class Front(NamedTuple):
    d: Any
    loaded: Any
    ut: Any
    v: Hops
    e: Any
    ehl: Any
    fhl: Any
    bl: Any
    ysum: Sums
    bsum: Sums
    z: Hops
    kern: Link
    maps: Link


class Scan(NamedTuple):
    phi: Any
    phl: Any
    part: Link
    rows: Link
    state: Link


class Route(NamedTuple):
    rows: Link
    cols: Link


class Rest(NamedTuple):
    first: Link
    swap: Link
    sel_s: Any
    sel_st: Any
    sel_r: Any
    sel_rt: Any
    rt: Any
    rpt: Any
    rpb: Any
    y: Any
    yb: Any
    mskt: Any
    fac: Any


def link(src, dst, count, kind=BF16):
    source = None if src is None else pltpu.VMEM(src, kind)
    return Link(source, pltpu.VMEM(dst, kind), DMA((count,)), DMA((count,)))


def sums(subs, rows, lanes):
    two, one = (2 * subs, rows, lanes), (subs, rows, lanes)
    return Sums(link(two, two, 2 * subs), link(one, one, subs), pltpu.VMEM(one, F32))


def front(count):
    return Front(
        d=pltpu.VMEM((COLS, NLOC, NLOC), BF16),
        loaded=DMA((COLS,)),
        ut=pltpu.VMEM((NLOC, RANK), BF16),
        v=Hops(pltpu.VMEM((COLS, RANK, NLOC), BF16), DMA((3, 1)), DMA((3, 1))),
        e=pltpu.VMEM((RANK, NLOC), F32),
        ehl=pltpu.VMEM((2 * RANK, NLOC), BF16),
        fhl=pltpu.VMEM((2 * RANK, NLOC), BF16),
        bl=pltpu.VMEM((NLOC, RANK), BF16),
        ysum=sums(SUBS, SUB, H),
        bsum=sums(1, NLOC // 2, 2 * RANK),
        z=Hops(pltpu.VMEM((COLS, SUBS, H, SUB), BF16), DMA((3, SUBS)), DMA((3, SUBS))),
        kern=link((COLS, RANK, 2 * RANK), (COLS, RANK, 2 * RANK), COLS),
        maps=link(None, (count, RANK, 2 * RANK), count, F32),
    )


def scan(count):
    part = (COLS, RANK // 2, 2 * HS)
    return Scan(
        phi=pltpu.VMEM((count * RANK // 2, 2 * RANK), F32),
        phl=pltpu.VMEM((4 * RANK, count * RANK // 2), BF16),
        part=link(part, part, COLS),
        rows=link(None, (count, RANK // 2, 2 * HS), count),
        state=link(None, part, COLS),
    )


def route(lanes):
    rows, cols = (ROWS, 32, lanes), (COLS, 128, lanes)
    return Route(link(rows, rows, ROWS), link(cols, cols, COLS))


def scratch_tree():
    part = (COLS, RANK // 2, 2 * HS)
    swap = (COLS, HS, NLOC)
    rest = Rest(
        first=link(None, part, COLS),
        swap=link(swap, swap, COLS),
        sel_s=pltpu.VMEM((ROWS * 32, 512), BF16),
        sel_st=pltpu.VMEM((512, ROWS * 32), BF16),
        sel_r=pltpu.VMEM((512, ROWS * 32), BF16),
        sel_rt=pltpu.VMEM((ROWS * 32, 512), BF16),
        rt=pltpu.VMEM((NLOC, H), BF16),
        rpt=pltpu.VMEM((NLOC, H), F32),
        rpb=pltpu.VMEM((NLOC, H), BF16),
        y=pltpu.VMEM((NLOC, H), F32),
        yb=pltpu.VMEM((NLOC, H), BF16),
        mskt=pltpu.VMEM((NLOC, RANK), BF16),
        fac=pltpu.VMEM((512, H), BF16),
    )
    return (
        front(HALF), front(ROWS), scan(ROWS), scan(ROWS), scan(HALF), route(H), route(BLK), route(H), rest,
    )


def dot(a, b):
    return jnp.dot(a, b, preferred_element_type=F32)


def dot_tn(a, b):
    return lax.dot_general(a, b, (((0,), (0,)), ((), ())), preferred_element_type=F32)


def dot_nt(a, b):
    return lax.dot_general(a, b, (((1,), (1,)), ((), ())), preferred_element_type=F32)


def high_low(a):
    high = a.astype(BF16)
    return high, (a - high.astype(F32)).astype(BF16)


def kernel(
    rc, rp, dc_hbm, dp_hbm, uc, vc, up, vp, pc, pp, msk, ws, tgt_row, tgt_col, src_row, src_col,
    xc_out, xp_out, child, parent, ahead, back, child_back, factors, weights, pulled, m,
):
    i = lax.axis_index("row")
    c = lax.axis_index("col")
    peer = c + 1 - 2 * lax.rem(c, 2)
    other = lax.rem(c + 2, COLS)
    diag = lax.rem(peer + 2, COLS)
    loc = lax.rem(i, HALF)
    base = i - loc
    dests = (diag, other, peer, c)
    pending = []

    def remote(src, dst, ss, rs, row, col):
        return pltpu.make_async_remote_copy(
            src_ref=src, dst_ref=dst, send_sem=ss, recv_sem=rs, device_id=(row, col), device_id_type=MESH
        )

    def looped(lo, hi, fn):
        def one(s, carry):
            fn(s)
            return carry

        lax.fori_loop(lo, hi, one, 0)

    def piece_of(ln, here, to):
        return ln.dst.at[here] if ln.src is None else ln.src.at[to]

    def col_copy(ln, d, to, slot):
        return remote(piece_of(ln, c, to), ln.dst.at[slot], ln.sent.at[d], ln.came.at[d], i, to)

    def col_send(ln):
        for d in range(1, COLS):
            col_copy(ln, d, lax.rem(c + d, COLS), c).start()
        pending.append(lambda: [col_copy(ln, d, lax.rem(c + d, COLS), c).wait_send() for d in range(1, COLS)])

    def col_wait(ln):
        for d in range(1, COLS):
            frm = lax.rem(c - d + COLS, COLS)
            col_copy(ln, d, frm, frm).wait_recv()

    def row_place(ln):
        n = ln.dst.shape[0]
        return (n, base, loc) if n == HALF else (n, 0, i)

    def row_copy(ln, d, to, slot):
        _, start, here = row_place(ln)
        return remote(piece_of(ln, here, to), ln.dst.at[slot], ln.sent.at[d], ln.came.at[d], start + to, c)

    def row_send(ln):
        n, _, here = row_place(ln)
        looped(1, n, lambda d: row_copy(ln, d, lax.rem(here + d, n), here).start())
        pending.append(
            lambda: looped(1, n, lambda d: row_copy(ln, d, lax.rem(here + d, n), here).wait_send())
        )

    def row_wait(ln):
        n, _, here = row_place(ln)

        def one(d):
            frm = lax.rem(here - d + n, n)
            row_copy(ln, d, frm, frm).wait_recv()

        looped(1, n, one)

    def hop(hops, step, s, whole=False):
        block = other if step == 2 else c
        to = other if step == 1 else peer
        ref = hops.buf.at[block] if whole else hops.buf.at[block, s]
        return remote(ref, ref, hops.sent.at[step, s], hops.came.at[step, s], i, to)

    def v_start(f, vbase):
        f.v.buf[c] = vbase[...]
        hop(f.v, 1, 0, True).start()
        hop(f.v, 0, 0, True).start()

    def v_forward(f):
        hop(f.v, 1, 0, True).wait_recv()
        hop(f.v, 2, 0, True).start()
        pending.append(lambda: [hop(f.v, step, 0, True).wait_send() for step in range(3)])

    def v_finish(f):
        hop(f.v, 0, 0, True).wait_recv()
        hop(f.v, 2, 0, True).wait_recv()

    def z_start(f, source):
        def one(s):
            piece = source[pl.ds(pl.multiple_of(s * SUB, SUB), SUB), :]
            f.z.buf[c, s] = piece.astype(F32).T.astype(BF16)
            hop(f.z, 1, s).start()
            hop(f.z, 0, s).start()

        looped(0, SUBS, one)
        pending.append(lambda: looped(0, SUBS, lambda s: [hop(f.z, step, s).wait_send() for step in range(3)] and None))

    def z_apply(f, block, out, step):
        def one(s):
            if step is not None:
                hop(f.z, step, s).wait_recv()
                if step == 1:
                    hop(f.z, 2, s).start()
            out[...] += dot(f.z.buf[block, s], f.d[block, pl.ds(pl.multiple_of(s * SUB, SUB), SUB), :])

        if step is None:
            out[...] = jnp.zeros(out.shape, F32)
        looped(0, SUBS, one)

    def within(sm, n):
        return remote(sm.a.src.at[n], sm.a.dst.at[n], sm.a.sent.at[n], sm.a.came.at[n], i, peer)

    def between(sm, n):
        return remote(sm.b.src.at[n], sm.b.dst.at[n], sm.b.sent.at[n], sm.b.came.at[n], i, other)

    def sum_away(sm, piece, ready=lambda n: None):
        subs = sm.acc.shape[0]
        ready(0)

        def first(s):
            sm.a.src[s] = piece(dests[0], s).astype(BF16)
            within(sm, s).start()

        looped(0, subs, first)
        ready(1)

        def second(s):
            own = piece(dests[1], s)
            within(sm, s).wait_recv()
            sm.b.src[s] = (own + sm.a.dst[s].astype(F32)).astype(BF16)
            between(sm, s).start()

        looped(0, subs, second)

    def sum_here(sm, piece):
        subs = sm.acc.shape[0]

        def third(s):
            sm.a.src[subs + s] = piece(dests[2], s).astype(BF16)
            within(sm, subs + s).start()

        looped(0, subs, third)

        def fourth(s):
            sm.acc[s] = piece(dests[3], s)

        looped(0, subs, fourth)

        def each(s):
            within(sm, s).wait_send()
            within(sm, subs + s).wait_send()
            between(sm, s).wait_send()

        pending.append(lambda: looped(0, subs, each))

    def sum_wait(sm, s):
        subs = sm.acc.shape[0]
        within(sm, subs + s).wait_recv()
        between(sm, s).wait_recv()
        return sm.acc[s] + sm.a.dst[subs + s].astype(F32) + sm.b.dst[s].astype(F32)

    def d_piece(f, rhs):
        def piece(dest, s):
            return dot(f.d[dest, pl.ds(pl.multiple_of(s * SUB, SUB), SUB), :], rhs[...])

        return piece

    def b_piece(f):
        def piece(dest, s):
            out = dot(f.d[dest], f.ut[...])
            return jnp.concatenate([out[: NLOC // 2], out[NLOC // 2 :]], axis=1)

        return piece

    def b_finish(f):
        packed = sum_wait(f.bsum, 0)
        out = jnp.concatenate([packed[:, :RANK], packed[:, RANK:]], axis=0)
        f.bl[...] = out.astype(BF16)
        high, low = high_low(out.T)
        f.fhl[:RANK] = high
        f.fhl[RANK:] = low

    def make_e(f):
        def one(b):
            f.e[...] += dot(f.v.buf[b], f.d[b])

        f.e[...] = jnp.zeros((RANK, NLOC), F32)
        looped(0, COLS, one)
        high, low = high_low(f.e[...])
        f.ehl[:RANK] = high
        f.ehl[RANK:] = low

    def project(pair, vec):
        both = dot(pair[...], vec)
        return both[:RANK] + both[RANK:]

    def pack(a):
        return jnp.concatenate([a[: RANK // 2], a[RANK // 2 :]], axis=1)

    def unpack(a):
        return jnp.concatenate([a[:, :HS], a[:, HS:]], axis=0)

    def scan_one(sc, partial):
        for k in range(COLS):
            sc.part.src[k] = pack(partial[:, k * HS : (k + 1) * HS]).astype(BF16)
        col_send(sc.part)

    def scan_two(sc):
        sc.part.dst[c] = sc.part.src[c]
        col_wait(sc.part)
        sc.rows.dst[row_place(sc.rows)[2]] = jnp.sum(sc.part.dst[...].astype(F32), axis=0).astype(BF16)
        row_send(sc.rows)

    def scan_three(sc):
        row_wait(sc.rows)
        both = dot(sc.phl[...], sc.rows.dst[...].reshape(sc.phl.shape[1], 2 * HS))
        both = both[: 2 * RANK] + both[2 * RANK :]
        send_state(sc.state, both[:RANK, :HS] + both[RANK:, HS:])

    def send_state(ln, state):
        ln.dst[c] = pack(state).astype(BF16)
        col_send(ln)

    def wait_state(ln):
        col_wait(ln)
        return jnp.concatenate([unpack(ln.dst[k].astype(F32)) for k in range(COLS)], axis=1).astype(BF16)

    def split_phi(sc):
        high, low = high_low(sc.phi[...].T)
        sc.phl[: 2 * RANK] = high
        sc.phl[2 * RANK :] = low

    def kernel_send(f, kernel_part, source):
        for k in range(COLS):
            left = kernel_part if source is None else source[:, k * HS : (k + 1) * HS]
            f.kern.src[k] = jnp.concatenate([left, kernel_part], axis=1).astype(BF16)
        col_send(f.kern)

    def kernel_sum(f, trans):
        f.kern.dst[c] = f.kern.src[c]
        col_wait(f.kern)
        total = jnp.sum(f.kern.dst[...].astype(F32), axis=0)
        return total[:, :HS], trans[...] - total[:, HS:]

    def maps_send(f, left, right):
        f.maps.dst[row_place(f.maps)[2]] = jnp.concatenate([left, right], axis=1)
        row_send(f.maps)

    def route_rows(rt, values):
        rt.rows.src[...] = values.astype(BF16).reshape(rt.rows.src.shape)
        rt.rows.dst[i] = rt.rows.src[i]
        row_send(rt.rows)

    def route_cols(rt):
        rt.cols.dst[c] = rt.cols.src[c]
        col_send(rt.cols)

    def rows_of(rt):
        row_wait(rt.rows)
        return rt.rows.dst[...].reshape(ROWS * 32, rt.rows.dst.shape[2])

    def onehot(shape, axis, at):
        return (lax.broadcasted_iota(jnp.int32, shape, axis) == at[...]).astype(BF16)

    def load(f, hbm, n):
        return pltpu.make_async_copy(hbm.at[dests[n]], f.d.at[dests[n]], f.loaded.at[n])

    for n in range(COLS):
        load(child, dc_hbm, n).start()
    for n in range(COLS):
        load(parent, dp_hbm, n).start()

    barrier = pltpu.get_barrier_semaphore()

    def greet(row, col):
        pl.semaphore_signal(barrier, inc=1, device_id=(row, col), device_id_type=MESH)

    looped(1, ROWS, lambda d: greet(lax.rem(i + d, ROWS), c))
    for d in range(1, COLS):
        greet(i, lax.rem(c + d, COLS))

    for s in range(SUBS):
        m.rt[s * SUB : (s + 1) * SUB, :] = rc[:, s * SUB : (s + 1) * SUB].T.astype(BF16)
    child.ut[...] = uc[...].astype(F32).T.astype(BF16)
    parent.ut[...] = up[...].astype(F32).T.astype(BF16)
    pl.semaphore_wait(barrier, ROWS + COLS - 2)

    v_start(child, vc)
    y_part = d_piece(child, m.rt)
    sum_away(child.ysum, y_part, lambda n: load(child, dc_hbm, n).wait())
    v_forward(child)
    load(child, dc_hbm, 2).wait()
    load(child, dc_hbm, 3).wait()
    v_finish(child)
    make_e(child)
    kernel_send(child, project(child.ehl, child.ut[...]), project(child.ehl, m.rt[...]))
    sum_here(child.ysum, y_part)
    source, transfer = kernel_sum(child, pc)
    maps_send(child, transfer, source)
    sum_away(child.bsum, b_piece(child))
    sum_here(child.bsum, b_piece(child))

    m.sel_s[...] = onehot((ROWS * 32, 512), 0, tgt_row)
    route_rows(weights, dot(m.sel_s[...], ws[...]))

    row_wait(child.maps)
    eye = (
        lax.broadcasted_iota(jnp.int32, (RANK, RANK), 0) == lax.broadcasted_iota(jnp.int32, (RANK, RANK), 1)
    ).astype(F32)
    left = lax.broadcasted_iota(jnp.int32, (RANK, 2 * RANK), 1) < RANK

    def store_phi(sc, j, value):
        sc.phi[pl.ds(pl.multiple_of(j * (RANK // 2), RANK // 2), RANK // 2), :] = pack(value)

    def child_step(j, both):
        now = child.maps.dst[j]
        product = jnp.dot(now[:, :RANK], both, precision=HIGH)
        added = jnp.concatenate([now[:, RANK:], jnp.zeros((RANK, RANK), F32)], axis=1)
        store_phi(child_back, j, jnp.where(j > loc, both[:, RANK:], 0.0))
        moves = (left & (j < loc)) | (~left & (j > loc))
        return jnp.where(moves, product + added, both)

    both = lax.fori_loop(
        0, HALF, child_step, jnp.concatenate([jnp.zeros((RANK, RANK), F32), eye], axis=1)
    )
    send_state(m.first, both[:, :RANK])
    b_finish(child)
    h_child = wait_state(m.first)

    def child_y(s):
        rows = pl.ds(pl.multiple_of(s * SUB, SUB), SUB)
        value = sum_wait(child.ysum, s) - dot(child.bl[rows, :], h_child)
        m.y[rows, :] = value
        m.yb[rows, :] = value.astype(BF16)

    looped(0, SUBS, child_y)
    for g in range(GROUPS):
        m.fac[g * RANK : (g + 1) * RANK, :] = dot(
            msk[:, g * BLK : (g + 1) * BLK], m.yb[g * BLK : (g + 1) * BLK, :]
        ).astype(BF16)
    route_rows(factors, dot(m.sel_s[...], m.fac[...]))

    v_start(parent, vp)
    for k in range(COLS):
        m.swap.src[k] = rp[:, k * NLOC : (k + 1) * NLOC].astype(BF16)
    m.swap.dst[c] = m.swap.src[c]
    col_send(m.swap)
    for n in range(COLS):
        load(parent, dp_hbm, n).wait()
    sum_away(parent.bsum, b_piece(parent))
    v_forward(parent)
    sum_here(parent.bsum, b_piece(parent))
    v_finish(parent)
    make_e(parent)
    kernel_send(parent, project(parent.ehl, parent.ut[...]), None)
    m.sel_r[...] = onehot((512, ROWS * 32), 1, src_col)
    weights.cols.src[...] = dot(m.sel_r[...], rows_of(weights)).astype(BF16).reshape(COLS, 128, BLK)
    route_cols(weights)
    _, transfer = kernel_sum(parent, pp)
    maps_send(parent, transfer, transfer.T)
    m.sel_rt[...] = onehot((ROWS * 32, 512), 0, src_row)
    m.sel_st[...] = onehot((512, ROWS * 32), 1, tgt_col)
    split_phi(child_back)
    m.mskt[...] = msk[...].astype(F32).T.astype(BF16)
    col_wait(m.swap)
    for k in range(SUBS):
        cols = slice(k * SUB, (k + 1) * SUB)
        m.rpt[cols, :] = m.swap.dst[:, :, cols].astype(F32).reshape(H, SUB).T
    b_finish(parent)
    row_wait(parent.maps)

    def parent_step(n, pair):
        rising, falling = pair
        j = ROWS - 1 - n
        store_phi(back, n, jnp.where(n > i, rising, 0.0))
        store_phi(ahead, j, jnp.where(j < i, falling, 0.0))
        up_next = jnp.dot(parent.maps.dst[n][:, :RANK], rising, precision=HIGH)
        down_next = jnp.dot(parent.maps.dst[j][:, RANK:], falling, precision=HIGH)
        return jnp.where(n > i, up_next, rising), jnp.where(j < i, down_next, falling)

    lax.fori_loop(0, ROWS, parent_step, (eye, eye))
    split_phi(ahead)
    split_phi(back)
    col_wait(weights.cols)

    factors.cols.src[...] = dot(m.sel_r[...], rows_of(factors)).astype(BF16).reshape(COLS, 128, H)
    route_cols(factors)
    col_wait(factors.cols)

    def joined(ref, q):
        return jnp.concatenate([ref[k, q * 16 : (q + 1) * 16, :] for k in range(COLS)], axis=0)

    for q in range(GROUPS):
        rows = slice(q * BLK, (q + 1) * BLK)
        contrib = dot_tn(joined(weights.cols.dst, q), joined(factors.cols.dst, q))
        m.rpb[rows, :] = (m.rpt[rows, :] - contrib).astype(BF16)

    scan_one(ahead, project(parent.ehl, m.rpb[...]))
    y_part = d_piece(parent, m.rpb)
    sum_away(parent.ysum, y_part)
    scan_two(ahead)
    sum_here(parent.ysum, y_part)
    scan_three(ahead)
    h_parent = wait_state(ahead.state)

    def parent_y(s):
        rows = pl.ds(pl.multiple_of(s * SUB, SUB), SUB)
        m.rpb[rows, :] = (sum_wait(parent.ysum, s) - dot(parent.bl[rows, :], h_parent)).astype(BF16)

    looped(0, SUBS, parent_y)
    z_start(parent, m.rpb)
    scan_one(back, project(parent.fhl, m.rpb[...]))
    z_apply(parent, c, xp_out, None)
    scan_two(back)
    z_apply(parent, peer, xp_out, 0)
    z_apply(parent, other, xp_out, 1)
    scan_three(back)
    z_apply(parent, diag, xp_out, 2)
    g_parent = wait_state(back.state)
    xp_out[...] -= dot_tn(g_parent, parent.ehl[:RANK])

    for q in range(GROUPS):
        values = dot_nt(joined(weights.cols.dst, q), xp_out[:, q * BLK : (q + 1) * BLK].astype(BF16)).astype(BF16)
        for k in range(COLS):
            pulled.cols.src[k, q * 16 : (q + 1) * 16, :] = values[k * 16 : (k + 1) * 16]
    route_cols(pulled)
    col_wait(pulled.cols)
    route_rows(pulled, dot(m.sel_rt[...], pulled.cols.dst[...].reshape(512, H)))
    m.fac[...] = dot(m.sel_st[...], rows_of(pulled)).astype(BF16)
    for g in range(GROUPS):
        rows = slice(g * BLK, (g + 1) * BLK)
        correction = dot(m.mskt[rows, :], m.fac[g * RANK : (g + 1) * RANK, :])
        m.yb[rows, :] = (m.y[rows, :] - correction).astype(BF16)

    z_start(child, m.yb)
    scan_one(child_back, project(child.fhl, m.yb[...]))
    z_apply(child, c, xc_out, None)
    scan_two(child_back)
    z_apply(child, peer, xc_out, 0)
    z_apply(child, other, xc_out, 1)
    scan_three(child_back)
    z_apply(child, diag, xc_out, 2)
    g_child = wait_state(child_back.state)
    xc_out[...] -= dot_tn(g_child, child.ehl[:RANK])
    for done in pending:
        done()


def shards(
    rhs_child, rhs_parent, dinv_child, dinv_parent, ubase_child, vbase_child, ubase_parent, vbase_parent,
    trans_child, trans_parent, w_first, w_second, block_ranks, extend_map,
):
    i = lax.axis_index("row")
    c = lax.axis_index("col")
    allowed = jnp.arange(RANK, dtype=jnp.int32)[:, None] < jnp.repeat(block_ranks, BLK)[None, :]
    masked = jnp.where(allowed, w_first, jnp.zeros_like(w_first))
    second = lax.dynamic_slice_in_dim(w_second, c * GROUPS, GROUPS, 0)
    second = second.reshape(GROUPS * RANK, BLK)

    entries = extend_map.reshape(ROWS, RANK)
    target = entries // 32
    serial = jnp.arange(RANK, dtype=jnp.int32)
    same = (target[:, :, None] == target[:, None, :]) & (serial[None, None, :] < serial[None, :, None])
    count = jnp.sum(same, axis=2, dtype=jnp.int32)
    groups = jnp.arange(GROUPS, dtype=jnp.int32) * SLOTS
    tgt = (lax.dynamic_index_in_dim(target * 32 + count, i, 0, False)[None, :] + groups[:, None]).reshape(-1)
    code = (jnp.arange(ROWS, dtype=jnp.int32)[:, None] * 32 + count).reshape(1, 2, -1)
    found = entries.reshape(1, 2, -1) == (i * 32 + jnp.arange(32, dtype=jnp.int32))[:, None, None]
    src = jnp.sum(jnp.where(found, code, 0), axis=2, dtype=jnp.int32)
    src = (src[:, :, None] + groups[None, None, :]).reshape(-1)

    vmem = pl.BlockSpec(memory_space=pltpu.VMEM)
    hbm = pl.BlockSpec(memory_space=pl.ANY)
    return tuple(
        pl.pallas_call(
            kernel,
            out_shape=[jax.ShapeDtypeStruct((H, NLOC), F32)] * 2,
            in_specs=[vmem, vmem, hbm, hbm] + [vmem] * 12,
            out_specs=[vmem, vmem],
            scratch_shapes=scratch_tree(),
            compiler_params=pltpu.CompilerParams(
                collective_id=0, has_side_effects=True, vmem_limit_bytes=60 * 1024 * 1024
            ),
        )(
            rhs_child,
            rhs_parent,
            dinv_child.reshape(COLS, NLOC, NLOC),
            dinv_parent.reshape(COLS, NLOC, NLOC),
            ubase_child,
            vbase_child,
            ubase_parent,
            vbase_parent,
            trans_child.reshape(RANK, RANK),
            trans_parent.reshape(RANK, RANK),
            masked,
            second,
            tgt[None, :],
            tgt[:, None],
            src[None, :],
            src[:, None],
        )
    )


def solution(mesh):
    return jax.shard_map(
        shards,
        mesh=mesh,
        in_specs=(
            P(None, ("row", "col")),
            P("col", "row"),
            P("row", "col"),
            P("row", "col"),
            P(None, ("row", "col")),
            P(None, ("row", "col")),
            P(None, ("row", "col")),
            P(None, ("row", "col")),
            P("row", None, None),
            P("row", None, None),
            P(None, ("row", "col")),
            P(None, "row"),
            P(("row", "col")),
            P(),
        ),
        out_specs=(P(None, ("row", "col")), P(None, ("row", "col"))),
        check_vma=False,
    )
```

time: 944 us -> 206 us (0.22); the launches traced: 926 us -> 206 us
  blocking collectives: 494 us -> 0 us
  waiting for transfers between devices: 202 us -> 0 us
  Pallas kernels: 0 us -> 191 us
  matrix products: 120 us -> 0 us
  starting transfers between devices: 54.6 us -> 0 us
  local copies, waits for them, and re-layouts: 27.6 us -> 11 us
  between operations: 14.7 us -> 0.71 us
    all_gather x4 -> x0, blocking collectives: 371 us -> none  [prefix_2(): gathered = jax.tree.map(lambda a: lax.all_gather(a, axis), part)]
    pallas_call x0 -> x1, Pallas kernels: none -> 191 us  [shards(): pl.pallas_call(kernel, out_shape=[jax.ShapeDtypeStruct((H, NLOC), F32)] *...]
    dot_general x86 -> x0, matrix products: 120 us -> none  [the longest x62 65 us: compose(): jnp.dot(after_pair[0], before_pair[1], precision=PRECISE) + after_pair[1]]
    all_gather x6 -> x0, waiting for transfers between devices: 106 us -> none  [the longest x2 106 us: gather_apply(): lax.all_gather(stacked, 'col', axis=1, tiled=True)]
    all_to_all x4 -> x0, blocking collectives: 81.3 us -> none  [the longest x3 47.3 us: column_swap(): lax.all_to_all(pieces, 'col', split_axis=0, concat_axis=1, tiled=True)]
    reduce_scatter x2 -> x0, waiting for transfers between devices: 65.1 us -> none  [sum_apply(): lax.psum_scatter(lax.dot_general(matrix, stacked, (((1,), (1,)), ((), ())...]
    all_to_all x2 -> x0, starting transfers between devices: 54.1 us -> none  [the longest x1 35.4 us: extend_swap(): lax.all_to_all(bucket_contents, 'row', split_axis=0, concat_axis=0, tiled...]
    psum x4 -> x0, blocking collectives: 42.3 us -> none  [column_sums(): lax.psum(second_term.astype(jnp.bfloat16), 'col').astype(jnp.float32)]
  transfers between devices with their start and end apart: 10 -> 0, of which waited for: 6 -> 0; matrix products, arithmetic and copies ran while one was open for 0% -> 0% of each run, Pallas kernels for 0% -> 0%
where the time goes in v1:
time: 206 us
  Pallas kernels  191 us (93%)
  local copies, waits for them, and re-layouts  11 us (5%)
  other arithmetic  2.94 us (1%)
    pallas_call x1, Pallas kernels, shards(): pl.pallas_call(kernel, out_shape=[jax.ShapeDtypeStruct((H, NLOC), F32)] *...  191 us
    unnamed x4, local copies, waits for them, and re-layouts  4.62 us

profile of v1, /device:TPU:1, one launch (start us, length us, event | category | flops | bytes accessed | tf_op | source)
XLA Modules:
  0.0 205.9 jit_solution(5907266668106122265)
XLA Ops:
  0.6 0.0 copy-start
  0.7 0.8 broadcast_bitcast_fusion
  1.5 0.7 eq.31
  2.2 0.1 add.123
  2.2 0.1 add.124
  2.3 0.8 reshape.221
  3.1 0.9 convert_reduce_fusion
  4.1 0.1 reduce_sum.21
  4.2 0.2 select_reduce_fusion
  4.4 0.1 broadcast_add_fusion.1
  4.4 0.7 add.119.tgt_row
  5.1 0.1 copy.18
  5.2 0.1 broadcast_add_fusion
  5.3 0.7 add.129.src_row
  6.0 1.6 fusion.msk
  7.6 0.0 copy-done
  7.6 0.7 reshape.220.ws
  8.3 0.9 add.132.src_col
  9.2 0.9 add.131.tgt_col
  10.1 191.2 %shard_map.149 = (f32[256,1024]{1,0:T(8,128)}, f32[256,1024]{1,0:T(8,128)}) custom-call(f32[256,1024]{1,0:T(8,128)} %rc.1, f32[64,4096]{1,0:T(8,128)} %rp.1, bf16[4,1024,1024]{2,1,0:T(8,128)(2,1)} %bitcast.8, bf16[4,1024,1024]{2,1,0:T(8,128)(2,1)} %bitcast.9, bf16[64,1024]{1,0:T(8,128)(2,1)} %uc.1, bf16[64,1024]{1,0:T(8,128)(2,1)} %vc.1, ...), custom_call_target="tpu_custom_call" | custom-call | tf_op jit(solution)/shard_map/pallas_call | solution.py:652
  201.3 2.3 %copy.23 = f32[256,1024]{1,0:T(8,128)} copy(f32[256,1024]{1,0:T(8,128)} %get-tuple-element.4) | data formatting | bytes 2097152
  203.6 2.3 %copy.24 = f32[256,1024]{1,0:T(8,128)} copy(f32[256,1024]{1,0:T(8,128)} %get-tuple-element.5) | data formatting | bytes 2097152
  (8 shorter events, 0.1 us)
Async XLA Ops:
  0.6 7.0 %copy-start = (bf16[32,8192]{1,0:T(8,128)(2,1)S(1)}, bf16[32,8192]{1,0:T(8,128)(2,1)}, u32[]{:S(2)}) copy-start(bf16[32,8192]{1,0:T(8,128)(2,1)} %param.25) | copy-start | bytes 1572868

commit v2 on v1

v2 whole, which is shorter than its diff:
```python
from typing import Any, NamedTuple

import jax
import jax.numpy as jnp
from jax import lax
from jax.experimental import pallas as pl
from jax.experimental.pallas import tpu as pltpu
from jax.sharding import PartitionSpec as P

MESH = pl.DeviceIdType.MESH
F32 = jnp.float32
BF16 = jnp.bfloat16
HIGH = lax.Precision.HIGHEST

ROWS = 32
COLS = 4
HALF = 16
H = 256
HS = 64
RANK = 64
NLOC = 1024
GROUPS = 8
BLK = 128
SUBS = 4
SUB = NLOC // SUBS
SLOTS = 4

DMA = pltpu.SemaphoreType.DMA


class Link(NamedTuple):
    src: Any
    dst: Any
    sent: Any
    came: Any


class Hops(NamedTuple):
    buf: Any
    sent: Any
    came: Any


class Sums(NamedTuple):
    a: Link
    b: Link


class Front(NamedTuple):
    d: Any
    loaded: Any
    ut: Any
    v: Hops
    e: Any
    ehl: Any
    fhl: Any
    bl: Any
    ysum: Sums
    bsum: Sums
    z: Hops
    kern: Link
    maps: Link


class Scan(NamedTuple):
    phi: Any
    phl: Any
    part: Link
    rows: Link
    state: Link


class Route(NamedTuple):
    rows: Link
    cols: Link


class Rest(NamedTuple):
    first: Link
    swap: Link
    sel_tall: Any
    sel_wide: Any
    held: Any
    acc: Any
    bacc: Any
    rt: Any
    rpt: Any
    rpb: Any
    y: Any
    yb: Any
    mskt: Any
    fac: Any
    msk: Any
    trans: Link
    rc: Any
    rp: Any
    w16: Any
    xp: Any
    near: Any


def link(src, dst, count, kind=BF16):
    source = None if src is None else pltpu.VMEM(src, kind)
    return Link(source, pltpu.VMEM(dst, kind), DMA((count,)), DMA((count,)))


def sums(subs, rows, lanes):
    two, one = (2 * subs, rows, lanes), (subs, rows, lanes)
    return Sums(link(two, two, 2 * subs), link(one, one, subs))


def front(count, tile):
    return Front(
        d=pltpu.VMEM((COLS, NLOC, NLOC), BF16),
        loaded=DMA((COLS,)),
        ut=pltpu.VMEM((NLOC, RANK), BF16),
        v=Hops(pltpu.VMEM((COLS, RANK, NLOC), BF16), DMA((3, 1)), DMA((3, 1))),
        e=pltpu.VMEM((RANK, NLOC), F32),
        ehl=pltpu.VMEM((2 * RANK, NLOC), BF16),
        fhl=pltpu.VMEM((2 * RANK, NLOC), BF16),
        bl=pltpu.VMEM((NLOC, RANK), BF16),
        ysum=sums(SUBS, SUB, H),
        bsum=sums(1, NLOC // 2, 2 * RANK),
        z=Hops(pltpu.VMEM((COLS, SUBS, H, SUB), BF16), DMA((3, SUBS)), DMA((3, SUBS))),
        kern=link((COLS, RANK, 2 * RANK), (2 * COLS, RANK, 2 * RANK), 2 * COLS),
        maps=link(None, (count // 2, 2) + tile, count // 2, F32),
    )


def scan(count):
    part = (RANK // 2, 2 * HS)
    return Scan(
        phi=pltpu.VMEM((count * RANK // 2, 2 * RANK), F32),
        phl=pltpu.VMEM((4 * RANK, count * RANK // 2), BF16),
        part=link((COLS,) + part, (2 * COLS,) + part, 2 * COLS),
        rows=link(None, (count // 2, 2) + part, count // 2),
        state=link(None, (COLS,) + part, COLS),
    )


def route(lanes):
    rows, cols = (ROWS, 32, lanes), (COLS, 128, lanes)
    return Route(link(rows, rows, ROWS), link(cols, cols, COLS))


def scratch_tree():
    part = (COLS, RANK // 2, 2 * HS)
    swap = (COLS, HS, NLOC)
    rest = Rest(
        first=link(None, part, COLS),
        swap=link(swap, swap, COLS),
        sel_tall=pltpu.VMEM((ROWS * 32, 512), BF16),
        sel_wide=pltpu.VMEM((512, ROWS * 32), BF16),
        held=pltpu.VMEM((SUBS, SUB, H), F32),
        acc=pltpu.VMEM((SUBS, SUB, H), F32),
        bacc=pltpu.VMEM((1, NLOC // 2, 2 * RANK), F32),
        rt=pltpu.VMEM((NLOC, H), BF16),
        rpt=pltpu.VMEM((NLOC, H), F32),
        rpb=pltpu.VMEM((NLOC, H), BF16),
        y=pltpu.VMEM((NLOC, H), F32),
        yb=pltpu.VMEM((NLOC, H), BF16),
        mskt=pltpu.VMEM((NLOC, RANK), BF16),
        fac=pltpu.VMEM((512, H), BF16),
        msk=pltpu.VMEM((RANK, NLOC), BF16),
        trans=link(None, (2, RANK, 2 * RANK), 1, F32),
        rc=pltpu.VMEM((H, NLOC), F32),
        rp=pltpu.VMEM((HS, COLS * NLOC), F32),
        w16=pltpu.VMEM((2 * GROUPS, RANK * BLK), BF16),
        xp=pltpu.VMEM((H, NLOC), F32),
        near=DMA((8,)),
    )
    return (
        front(HALF, (RANK, 2 * RANK)), front(ROWS, (RANK // 2, 2 * RANK)), scan(ROWS), scan(ROWS), scan(HALF), route(H), route(BLK), route(H), rest,
    )


def dot(a, b):
    return jnp.dot(a, b, preferred_element_type=F32)


def dot_tn(a, b):
    return lax.dot_general(a, b, (((0,), (0,)), ((), ())), preferred_element_type=F32)


def dot_nt(a, b):
    return lax.dot_general(a, b, (((1,), (1,)), ((), ())), preferred_element_type=F32)


def high_low(a):
    high = a.astype(BF16)
    return high, (a - high.astype(F32)).astype(BF16)


def kernel(
    rc_hbm, rp_hbm, dc_hbm, dp_hbm, w_hbm, uc, vc, up, vp, wf, pc, pp, entries, ranks,
    xc_out, xp_out, child, parent, ahead, back, child_back, factors, weights, pulled, m,
):
    i = lax.axis_index("row")
    c = lax.axis_index("col")
    peer = c + 1 - 2 * lax.rem(c, 2)
    other = lax.rem(c + 2, COLS)
    diag = lax.rem(peer + 2, COLS)
    loc = lax.rem(i, HALF)
    base = i - loc
    side = lax.rem(i, 2)
    twin = i + 1 - 2 * side
    dests = (diag, other, peer, c)
    pending = []

    def remote(src, dst, ss, rs, row, col):
        return pltpu.make_async_remote_copy(
            src_ref=src, dst_ref=dst, send_sem=ss, recv_sem=rs, device_id=(row, col), device_id_type=MESH
        )

    def looped(lo, hi, fn):
        def one(s, carry):
            fn(s)
            return carry

        lax.fori_loop(lo, hi, one, 0)

    def piece_of(ln, here, to):
        return ln.dst.at[here] if ln.src is None else ln.src.at[to]

    def col_copy(ln, d, to, slot):
        return remote(piece_of(ln, c, to), ln.dst.at[slot], ln.sent.at[d], ln.came.at[d], i, to)

    def col_send(ln):
        for d in range(1, COLS):
            col_copy(ln, d, lax.rem(c + d, COLS), c).start()
        pending.append(lambda: [col_copy(ln, d, lax.rem(c + d, COLS), c).wait_send() for d in range(1, COLS)])

    def col_wait(ln):
        for d in range(1, COLS):
            frm = lax.rem(c - d + COLS, COLS)
            col_copy(ln, d, frm, frm).wait_recv()

    def row_place(ln):
        n = ln.dst.shape[0]
        return (n, base, loc) if n == HALF else (n, 0, i)

    def row_copy(ln, d, to, slot):
        _, start, here = row_place(ln)
        return remote(piece_of(ln, here, to), ln.dst.at[slot], ln.sent.at[d], ln.came.at[d], start + to, c)

    def row_send(ln):
        n, _, here = row_place(ln)
        looped(1, n, lambda d: row_copy(ln, d, lax.rem(here + d, n), here).start())
        pending.append(
            lambda: looped(1, n, lambda d: row_copy(ln, d, lax.rem(here + d, n), here).wait_send())
        )

    def row_wait(ln):
        n, _, here = row_place(ln)

        def one(d):
            frm = lax.rem(here - d + n, n)
            row_copy(ln, d, frm, frm).wait_recv()

        looped(1, n, one)

    def twin_copy(ln, n, to, slot, row):
        return remote(ln.src.at[to], ln.dst.at[slot], ln.sent.at[n], ln.came.at[n], row, to)

    def twin_send(ln):
        for d in range(1, COLS):
            twin_copy(ln, d, lax.rem(c + d, COLS), side * COLS + c, i).start()
        for d in range(COLS):
            twin_copy(ln, COLS + d, lax.rem(c + d, COLS), side * COLS + c, twin).start()

        def done():
            for d in range(1, COLS):
                twin_copy(ln, d, lax.rem(c + d, COLS), side * COLS + c, i).wait_send()
            for d in range(COLS):
                twin_copy(ln, COLS + d, lax.rem(c + d, COLS), side * COLS + c, twin).wait_send()

        pending.append(done)

    def twin_wait(ln):
        ln.dst[side * COLS + c] = ln.src[c]
        for d in range(1, COLS):
            frm = lax.rem(c - d + COLS, COLS)
            twin_copy(ln, d, frm, side * COLS + frm, i).wait_recv()
        for d in range(COLS):
            frm = lax.rem(c - d + COLS, COLS)
            twin_copy(ln, COLS + d, frm, (1 - side) * COLS + frm, twin).wait_recv()
        return [jnp.sum(ln.dst[k * COLS : (k + 1) * COLS].astype(F32), axis=0) for k in range(2)]

    def pair_place(ln):
        n = ln.dst.shape[0]
        return (n, base, lax.div(loc, 2)) if n == HALF // 2 else (n, 0, lax.div(i, 2))

    def pair_copy(ln, d, to, slot):
        _, start, here = pair_place(ln)
        return remote(
            ln.dst.at[here], ln.dst.at[slot], ln.sent.at[d], ln.came.at[d], start + 2 * to + side, c
        )

    def pair_send(ln):
        n, _, here = pair_place(ln)
        looped(1, n, lambda d: pair_copy(ln, d, lax.rem(here + d, n), here).start())
        pending.append(
            lambda: looped(1, n, lambda d: pair_copy(ln, d, lax.rem(here + d, n), here).wait_send())
        )

    def pair_wait(ln):
        n, _, here = pair_place(ln)

        def one(d):
            frm = lax.rem(here - d + n, n)
            pair_copy(ln, d, frm, frm).wait_recv()

        looped(1, n, one)

    def hop(hops, step, s, whole=False):
        block = other if step == 2 else c
        to = other if step == 1 else peer
        ref = hops.buf.at[block] if whole else hops.buf.at[block, s]
        return remote(ref, ref, hops.sent.at[step, s], hops.came.at[step, s], i, to)

    def v_start(f, vbase):
        f.v.buf[c] = vbase[...]
        hop(f.v, 1, 0, True).start()
        hop(f.v, 0, 0, True).start()

    def v_forward(f):
        hop(f.v, 1, 0, True).wait_recv()
        hop(f.v, 2, 0, True).start()
        pending.append(lambda: [hop(f.v, step, 0, True).wait_send() for step in range(3)])

    def z_start(f, source):
        def one(s):
            piece = source[pl.ds(pl.multiple_of(s * SUB, SUB), SUB), :]
            f.z.buf[c, s] = piece.astype(F32).T.astype(BF16)
            hop(f.z, 0, s).start()

        def first(s):
            one(s)
            hop(f.z, 1, s).start()

        looped(0, SUBS - 1, first)
        one(SUBS - 1)

        def each(s):
            for step in range(3):
                hop(f.z, step, s).wait_send()

        pending.append(lambda: looped(0, SUBS, each))

    def z_apply(f, block, out, step):
        def one(s):
            if step is not None:
                hop(f.z, step, s).wait_recv()
                if step == 1:
                    hop(f.z, 2, s).start()
            out[...] += dot(f.z.buf[block, s], f.d[block, pl.ds(pl.multiple_of(s * SUB, SUB), SUB), :])

        if step is None:
            out[...] = jnp.zeros(out.shape, F32)
        looped(0, SUBS, one)

    def within(sm, n):
        return remote(sm.a.src.at[n], sm.a.dst.at[n], sm.a.sent.at[n], sm.a.came.at[n], i, peer)

    def between(sm, n):
        return remote(sm.b.src.at[n], sm.b.dst.at[n], sm.b.sent.at[n], sm.b.came.at[n], i, other)

    def a_pieces(sm, n, dest, piece):
        subs = sm.b.dst.shape[0]

        def one(p):
            out = piece(dest, p).astype(BF16)
            if subs == 1:
                sm.a.src[n] = out
            else:
                sm.a.src[n * subs + 2 * p] = out[:SUB]
                sm.a.src[n * subs + 2 * p + 1] = out[SUB:]

        looped(0, max(subs // 2, 1), one)

    def a_send(sm, n):
        subs = sm.b.dst.shape[0]
        looped(0, subs, lambda s: within(sm, n * subs + s).start())

    def own_pieces(sm, into, dest, piece):
        subs = sm.b.dst.shape[0]

        def one(p):
            out = piece(dest, p)
            if subs == 1:
                into[0] = out
            else:
                into[2 * p] = out[:SUB]
                into[2 * p + 1] = out[SUB:]

        looped(0, max(subs // 2, 1), one)

    def b_make(sm, held):
        def one(s):
            within(sm, s).wait_recv()
            sm.b.src[s] = (held[s] + sm.a.dst[s].astype(F32)).astype(BF16)

        looped(0, sm.b.dst.shape[0], one)

    def b_send(sm, lo, hi):
        looped(lo, hi, lambda s: between(sm, s).start())
        if hi == sm.b.dst.shape[0]:
            subs = hi

            def each(s):
                within(sm, s).wait_send()
                within(sm, subs + s).wait_send()
                between(sm, s).wait_send()

            pending.append(lambda: looped(0, subs, each))

    def b_sums(f):
        piece = b_piece(f)
        a_pieces(f.bsum, 0, diag, piece)
        a_send(f.bsum, 0)
        a_pieces(f.bsum, 1, peer, piece)
        a_send(f.bsum, 1)
        own_pieces(f.bsum, m.bacc, other, piece)
        b_make(f.bsum, m.bacc)
        b_send(f.bsum, 0, 1)
        own_pieces(f.bsum, m.bacc, c, piece)

    def sum_wait(sm, s):
        subs = sm.b.dst.shape[0]
        within(sm, subs + s).wait_recv()
        between(sm, s).wait_recv()
        acc = m.bacc if subs == 1 else m.acc
        return acc[s] + sm.a.dst[subs + s].astype(F32) + sm.b.dst[s].astype(F32)

    def d_piece(f, rhs):
        def piece(dest, s):
            return dot(f.d[dest, pl.ds(pl.multiple_of(s * 2 * SUB, 2 * SUB), 2 * SUB), :], rhs[...])

        return piece

    def b_piece(f):
        def piece(dest, s):
            out = dot(f.d[dest], f.ut[...])
            return jnp.concatenate([out[: NLOC // 2], out[NLOC // 2 :]], axis=1)

        return piece

    def b_finish(f):
        packed = sum_wait(f.bsum, 0)
        out = jnp.concatenate([packed[:, :RANK], packed[:, RANK:]], axis=0)
        f.bl[...] = out.astype(BF16)
        high, low = high_low(out.T)
        f.fhl[:RANK] = high
        f.fhl[RANK:] = low

    def make_e(f):
        def add(block):
            f.e[...] += dot(f.v.buf[block], f.d[block])

        f.e[...] = dot(f.v.buf[c], f.d[c])
        v_forward(f)
        add(other)
        hop(f.v, 0, 0, True).wait_recv()
        add(peer)
        hop(f.v, 2, 0, True).wait_recv()
        add(diag)
        high, low = high_low(f.e[...])
        f.ehl[:RANK] = high
        f.ehl[RANK:] = low

    def project(pair, vec):
        both = dot(pair[...], vec)
        return both[:RANK] + both[RANK:]

    def pack(a):
        return jnp.concatenate([a[: RANK // 2], a[RANK // 2 :]], axis=1)

    def unpack(a):
        return jnp.concatenate([a[:, :HS], a[:, HS:]], axis=0)

    def scan_one(sc, partial):
        for k in range(COLS):
            sc.part.src[k] = pack(partial[:, k * HS : (k + 1) * HS]).astype(BF16)
        twin_send(sc.part)

    def scan_two(sc):
        here = pair_place(sc.rows)[2]
        for k, total in enumerate(twin_wait(sc.part)):
            sc.rows.dst[here, k] = total.astype(BF16)
        pair_send(sc.rows)

    def scan_three(sc):
        pair_wait(sc.rows)
        both = dot(sc.phl[...], sc.rows.dst[...].reshape(sc.phl.shape[1], 2 * HS))
        both = both[: 2 * RANK] + both[2 * RANK :]
        send_state(sc.state, both[:RANK, :HS] + both[RANK:, HS:])

    def send_state(ln, state):
        ln.dst[c] = pack(state).astype(BF16)
        col_send(ln)

    def wait_state(ln):
        col_wait(ln)
        return jnp.concatenate([unpack(ln.dst[k].astype(F32)) for k in range(COLS)], axis=1).astype(BF16)

    def split_phi(sc):
        high, low = high_low(sc.phi[...].T)
        sc.phl[: 2 * RANK] = high
        sc.phl[2 * RANK :] = low

    def kernel_send(f, kernel_part, source):
        for k in range(COLS):
            left = kernel_part if source is None else source[:, k * HS : (k + 1) * HS]
            f.kern.src[k] = jnp.concatenate([left, kernel_part], axis=1).astype(BF16)
        twin_send(f.kern)

    def route_values(rt, values):
        rt.rows.src[...] = values.astype(BF16).reshape(rt.rows.src.shape)
        rt.rows.dst[i] = rt.rows.src[i]

    def route_rows(rt, values):
        route_values(rt, values)
        row_send(rt.rows)

    def route_cols(rt):
        rt.cols.dst[c] = rt.cols.src[c]
        col_send(rt.cols)

    def rows_of(rt):
        row_wait(rt.rows)
        return rt.rows.dst[...].reshape(ROWS * 32, rt.rows.dst.shape[2])

    def onehot(shape, axis, at):
        return (lax.broadcasted_iota(jnp.int32, shape, axis) == at).astype(BF16)

    def load(f, hbm, n):
        return pltpu.make_async_copy(hbm.at[dests[n]], f.d.at[dests[n]], f.loaded.at[n])

    load_rc = pltpu.make_async_copy(rc_hbm, m.rc, m.near.at[0])
    load_rp = pltpu.make_async_copy(rp_hbm, m.rp, m.near.at[1])
    load_w = pltpu.make_async_copy(
        w_hbm.at[pl.ds(pl.multiple_of(lax.div(c, 2) * 2 * GROUPS, 2 * GROUPS), 2 * GROUPS), :], m.w16, m.near.at[2]
    )
    load_rc.start()
    for n in range(COLS):
        load(child, dc_hbm, n).start()
    for n in range(COLS):
        load(parent, dp_hbm, n).start()
    load_w.start()
    load_rp.start()

    barrier = pltpu.get_barrier_semaphore()

    def greet(row, col):
        pl.semaphore_signal(barrier, inc=1, device_id=(row, col), device_id_type=MESH)

    looped(1, ROWS, lambda d: greet(lax.rem(i + d, ROWS), c))
    for d in range(1, COLS):
        greet(i, lax.rem(c + d, COLS))
        greet(twin, lax.rem(c + d, COLS))

    child.ut[...] = uc[...].astype(F32).T.astype(BF16)
    parent.ut[...] = up[...].astype(F32).T.astype(BF16)
    load_rc.wait()
    for s in range(SUBS):
        m.rt[s * SUB : (s + 1) * SUB, :] = m.rc[:, s * SUB : (s + 1) * SUB].T.astype(BF16)
    y_part = d_piece(child, m.rt)
    load(child, dc_hbm, 0).wait()
    a_pieces(child.ysum, 0, diag, y_part)
    load(child, dc_hbm, 1).wait()
    own_pieces(child.ysum, m.held, other, y_part)
    m.trans.dst[side] = jnp.concatenate([pc[...], pp[...]], axis=1)
    pl.semaphore_wait(barrier, ROWS - 1 + 2 * (COLS - 1))

    v_start(child, vc)
    v_start(parent, vp)
    trans_copy = remote(
        m.trans.dst.at[side], m.trans.dst.at[side], m.trans.sent.at[0], m.trans.came.at[0], twin, c
    )
    trans_from = remote(
        m.trans.dst.at[1 - side], m.trans.dst.at[1 - side], m.trans.sent.at[0], m.trans.came.at[0], twin, c
    )
    trans_copy.start()
    pending.append(trans_copy.wait_send)
    a_send(child.ysum, 0)
    load(child, dc_hbm, 2).wait()
    load(child, dc_hbm, 3).wait()
    make_e(child)
    kernel_send(child, project(child.ehl, child.ut[...]), project(child.ehl, m.rt[...]))
    a_pieces(child.ysum, 1, peer, y_part)
    a_send(child.ysum, 1)
    own_pieces(child.ysum, m.acc, c, y_part)
    b_make(child.ysum, m.held)
    trans_from.wait_recv()
    here = pair_place(child.maps)[2]
    for k, total in enumerate(twin_wait(child.kern)):
        transfer = m.trans.dst[k, :, :RANK] - total[:, RANK:]
        child.maps.dst[here, k] = jnp.concatenate([transfer, total[:, :RANK]], axis=1)
    pair_send(child.maps)
    b_send(child.ysum, 0, SUBS - 1)
    for n in range(COLS):
        load(parent, dp_hbm, n).wait()
    make_e(parent)
    kernel_send(parent, project(parent.ehl, parent.ut[...]), None)
    b_send(child.ysum, SUBS - 1, SUBS)
    b_sums(child)

    eye = (
        lax.broadcasted_iota(jnp.int32, (RANK, RANK), 0) == lax.broadcasted_iota(jnp.int32, (RANK, RANK), 1)
    )
    eye_f = eye.astype(F32)
    left = lax.broadcasted_iota(jnp.int32, (RANK, 2 * RANK), 1) < RANK

    def iota(rows, cols, axis):
        return lax.broadcasted_iota(jnp.int32, (rows, cols), axis)

    def over_lanes(mask, values):
        return jnp.sum(jnp.where(mask, values, 0), axis=1, keepdims=True)

    def over_rows(mask, values):
        return jnp.sum(jnp.where(mask, values, 0), axis=0, keepdims=True)

    mine = entries[pl.ds(i, 1), :] >> 5
    mine_col = over_lanes(eye, mine)
    earlier = (mine_col == mine) & (iota(RANK, RANK, 1) < iota(RANK, RANK, 0))
    tgt_col = mine_col * 32 + jnp.sum(earlier.astype(jnp.int32), axis=1, keepdims=True)
    tgt_row = over_rows(eye, tgt_col)
    wide = iota(RANK, 512, 1)
    tall = iota(512, RANK, 0)
    by_group = over_rows(iota(RANK, 512, 0) == (wide & (RANK - 1)), tgt_col) + 4 * (iota(1, 512, 1) >> 6)
    by_block = over_rows(iota(RANK, 512, 0) == (wide >> 3), tgt_col) + 4 * (iota(1, 512, 1) & 7)
    m.sel_tall[...] = onehot((ROWS * 32, 512), 0, by_block)
    load_w.wait()
    w16 = m.w16[...].astype(F32)
    w8 = jnp.where(lax.rem(c, 2) == 0, w16[:GROUPS], w16[GROUPS:])
    ws = jnp.concatenate([w8[:, b * BLK : (b + 1) * BLK] for b in range(RANK)], axis=0).astype(BF16)
    route_values(weights, dot(m.sel_tall[...], ws))
    m.sel_tall[...] = onehot((ROWS * 32, 512), 0, by_group)
    for g in range(GROUPS):
        cols = slice(g * BLK, (g + 1) * BLK)
        allowed = iota(RANK, BLK, 0) < ranks[g]
        m.msk[:, cols] = jnp.where(allowed, wf[:, cols].astype(F32), 0.0).astype(BF16)

    here = pair_place(parent.maps)[2]
    for k, total in enumerate(twin_wait(parent.kern)):
        parent.maps.dst[here, k] = pack(m.trans.dst[k, :, RANK:] - total[:, RANK:])
    pair_send(parent.maps)
    pair_wait(child.maps)
    row_send(weights.rows)

    def store_phi(sc, j, value):
        sc.phi[pl.ds(pl.multiple_of(j * (RANK // 2), RANK // 2), RANK // 2), :] = pack(value)

    def child_step(j, both):
        now = child.maps.dst[lax.div(j, 2), lax.rem(j, 2)]
        product = jnp.dot(now[:, :RANK], both, precision=HIGH)
        added = jnp.concatenate([now[:, RANK:], jnp.zeros((RANK, RANK), F32)], axis=1)
        store_phi(child_back, j, jnp.where(j > loc, both[:, RANK:], 0.0))
        moves = (left & (j < loc)) | (~left & (j > loc))
        return jnp.where(moves, product + added, both)

    both = lax.fori_loop(
        0, HALF, child_step, jnp.concatenate([jnp.zeros((RANK, RANK), F32), eye_f], axis=1)
    )
    send_state(m.first, both[:, :RANK])
    b_finish(child)
    h_child = wait_state(m.first)

    def child_y(s):
        rows = pl.ds(pl.multiple_of(s * SUB, SUB), SUB)
        value = sum_wait(child.ysum, s) - dot(child.bl[rows, :], h_child)
        m.y[rows, :] = value
        m.yb[rows, :] = value.astype(BF16)

    looped(0, SUBS, child_y)
    for g in range(GROUPS):
        m.fac[g * RANK : (g + 1) * RANK, :] = dot(
            m.msk[:, g * BLK : (g + 1) * BLK], m.yb[g * BLK : (g + 1) * BLK, :]
        ).astype(BF16)
    route_rows(factors, dot(m.sel_tall[...], m.fac[...]))

    load_rp.wait()
    for k in range(COLS):
        m.swap.src[k] = m.rp[:, k * NLOC : (k + 1) * NLOC].astype(BF16)
    m.swap.dst[c] = m.swap.src[c]
    col_send(m.swap)
    b_sums(parent)

    held_here = ((entries[...] >> 5) == i).astype(BF16)
    below = (iota(RANK, RANK, 0) < iota(RANK, RANK, 1)).astype(BF16)
    code = dot(held_here, below).astype(jnp.int32) + 32 * iota(ROWS, RANK, 0)
    wanted = i * 32 + (iota(RANK, RANK, 0) >> 1)
    second_half = iota(RANK, RANK, 0) & 1
    found = jnp.zeros((RANK, RANK), jnp.int32)
    for j in range(ROWS):
        hit = (entries[j : j + 1, :] == wanted) & (second_half == j // HALF)
        found = found + jnp.where(hit, code[j : j + 1, :], 0)
    src_col = jnp.sum(found, axis=1, keepdims=True)
    src_row = over_rows(eye, src_col)
    src_tall = over_lanes(iota(512, RANK, 1) == (tall >> 3), src_row) + 4 * (iota(512, 1, 0) & 7)
    src_wide = over_rows(iota(RANK, 512, 0) == (wide >> 3), src_col) + 4 * (iota(1, 512, 1) & 7)
    tgt_tall = over_lanes(iota(512, RANK, 1) == (tall & (RANK - 1)), tgt_row) + 4 * (iota(512, 1, 0) >> 6)
    m.sel_wide[...] = onehot((512, ROWS * 32), 1, src_tall)
    weights.cols.src[...] = dot(m.sel_wide[...], rows_of(weights)).astype(BF16).reshape(COLS, 128, BLK)
    route_cols(weights)
    pair_wait(parent.maps)

    def parent_step(n, pair):
        rising, falling = pair
        j = ROWS - 1 - n
        store_phi(back, n, jnp.where(n > i, rising, 0.0))
        store_phi(ahead, j, jnp.where(j < i, falling, 0.0).T)
        up_next = jnp.dot(unpack(parent.maps.dst[lax.div(n, 2), lax.rem(n, 2)]), rising, precision=HIGH)
        down_next = jnp.dot(falling, unpack(parent.maps.dst[lax.div(j, 2), lax.rem(j, 2)]), precision=HIGH)
        return jnp.where(n > i, up_next, rising), jnp.where(j < i, down_next, falling)

    lax.fori_loop(0, ROWS, parent_step, (eye_f, eye_f))
    split_phi(ahead)
    split_phi(back)
    split_phi(child_back)
    col_wait(m.swap)
    for k in range(SUBS):
        cols = slice(k * SUB, (k + 1) * SUB)
        m.rpt[cols, :] = m.swap.dst[:, :, cols].astype(F32).reshape(H, SUB).T
    b_finish(parent)
    col_wait(weights.cols)

    factors.cols.src[...] = dot(m.sel_wide[...], rows_of(factors)).astype(BF16).reshape(COLS, 128, H)
    route_cols(factors)
    m.mskt[...] = m.msk[...].astype(F32).T.astype(BF16)
    m.sel_tall[...] = onehot((ROWS * 32, 512), 0, src_wide)
    m.sel_wide[...] = onehot((512, ROWS * 32), 1, tgt_tall)
    col_wait(factors.cols)

    def joined(ref, q):
        return jnp.concatenate([ref[k, q * 16 : (q + 1) * 16, :] for k in range(COLS)], axis=0)

    for q in range(GROUPS):
        rows = slice(q * BLK, (q + 1) * BLK)
        contrib = dot_tn(joined(weights.cols.dst, q), joined(factors.cols.dst, q))
        m.rpb[rows, :] = (m.rpt[rows, :] - contrib).astype(BF16)

    scan_one(ahead, project(parent.ehl, m.rpb[...]))
    y_part = d_piece(parent, m.rpb)
    a_pieces(parent.ysum, 0, diag, y_part)
    a_send(parent.ysum, 0)
    own_pieces(parent.ysum, m.held, other, y_part)
    b_make(parent.ysum, m.held)
    b_send(parent.ysum, 0, SUBS - 1)
    scan_two(ahead)
    a_pieces(parent.ysum, 1, peer, y_part)
    a_send(parent.ysum, 1)
    own_pieces(parent.ysum, m.acc, c, y_part)
    scan_three(ahead)
    b_send(parent.ysum, SUBS - 1, SUBS)
    h_parent = wait_state(ahead.state)

    def parent_y(s):
        rows = pl.ds(pl.multiple_of(s * SUB, SUB), SUB)
        m.rpb[rows, :] = (sum_wait(parent.ysum, s) - dot(parent.bl[rows, :], h_parent)).astype(BF16)

    looped(0, SUBS, parent_y)
    scan_one(back, project(parent.fhl, m.rpb[...]))
    z_start(parent, m.rpb)
    z_apply(parent, c, m.xp, None)
    scan_two(back)
    z_apply(parent, peer, m.xp, 0)
    scan_three(back)
    hop(parent.z, 1, SUBS - 1).start()
    z_apply(parent, other, m.xp, 1)
    z_apply(parent, diag, m.xp, 2)
    g_parent = wait_state(back.state)
    m.xp[...] -= dot_tn(g_parent, parent.ehl[:RANK])
    store_xp = pltpu.make_async_copy(m.xp, xp_out, m.near.at[3])
    store_xp.start()
    pending.append(store_xp.wait)

    for q in range(GROUPS):
        values = dot_nt(joined(weights.cols.dst, q), m.xp[:, q * BLK : (q + 1) * BLK].astype(BF16)).astype(BF16)
        for k in range(COLS):
            pulled.cols.src[k, q * 16 : (q + 1) * 16, :] = values[k * 16 : (k + 1) * 16]
    route_cols(pulled)
    col_wait(pulled.cols)
    route_rows(pulled, dot(m.sel_tall[...], pulled.cols.dst[...].reshape(512, H)))
    m.fac[...] = dot(m.sel_wide[...], rows_of(pulled)).astype(BF16)
    for g in range(GROUPS):
        rows = slice(g * BLK, (g + 1) * BLK)
        correction = dot(m.mskt[rows, :], m.fac[g * RANK : (g + 1) * RANK, :])
        m.yb[rows, :] = (m.y[rows, :] - correction).astype(BF16)

    scan_one(child_back, project(child.fhl, m.yb[...]))
    z_start(child, m.yb)
    z_apply(child, c, m.rc, None)
    scan_two(child_back)
    z_apply(child, peer, m.rc, 0)
    scan_three(child_back)
    hop(child.z, 1, SUBS - 1).start()
    z_apply(child, other, m.rc, 1)
    z_apply(child, diag, m.rc, 2)
    g_child = wait_state(child_back.state)
    m.rc[...] -= dot_tn(g_child, child.ehl[:RANK])
    store_xc = pltpu.make_async_copy(m.rc, xc_out, m.near.at[4])
    store_xc.start()
    pending.append(store_xc.wait)
    for done in pending:
        done()


def hand_over(xc, xp, xc_out, xp_out):
    xc_out[...] = xc[...]
    xp_out[...] = xp[...]


def shards(
    rhs_child, rhs_parent, dinv_child, dinv_parent, ubase_child, vbase_child, ubase_parent, vbase_parent,
    trans_child, trans_parent, w_first, w_second, block_ranks, extend_map,
):
    vmem = pl.BlockSpec(memory_space=pltpu.VMEM)
    hbm = pl.BlockSpec(memory_space=pl.ANY)
    smem = pl.BlockSpec(memory_space=pltpu.SMEM)
    shapes = [jax.ShapeDtypeStruct((H, NLOC), F32)] * 2
    x_child, x_parent = pl.pallas_call(
        kernel,
        out_shape=shapes,
        in_specs=[hbm] * 5 + [vmem] * 8 + [smem],
        out_specs=[hbm, hbm],
        scratch_shapes=scratch_tree(),
        compiler_params=pltpu.CompilerParams(
            collective_id=0, has_side_effects=True, vmem_limit_bytes=60 * 1024 * 1024
        ),
    )(
        rhs_child,
        rhs_parent,
        dinv_child.reshape(COLS, NLOC, NLOC),
        dinv_parent.reshape(COLS, NLOC, NLOC),
        w_second,
        ubase_child,
        vbase_child,
        ubase_parent,
        vbase_parent,
        w_first,
        trans_child.reshape(RANK, RANK),
        trans_parent.reshape(RANK, RANK),
        extend_map.reshape(ROWS, RANK),
        block_ranks,
    )
    tile = pl.BlockSpec((H // 4, NLOC), lambda n: (n, 0))
    return tuple(
        pl.pallas_call(
            hand_over,
            grid=(4,),
            out_shape=shapes,
            in_specs=[tile, tile],
            out_specs=[tile, tile],
        )(x_child, x_parent)
    )


def solution(mesh):
    return jax.shard_map(
        shards,
        mesh=mesh,
        in_specs=(
            P(None, ("row", "col")),
            P("col", "row"),
            P("row", "col"),
            P("row", "col"),
            P(None, ("row", "col")),
            P(None, ("row", "col")),
            P(None, ("row", "col")),
            P(None, ("row", "col")),
            P("row", None, None),
            P("row", None, None),
            P(None, ("row", "col")),
            P(None, "row"),
            P(("row", "col")),
            P(),
        ),
        out_specs=(P(None, ("row", "col")), P(None, ("row", "col"))),
        check_vma=False,
    )
```

time: 206 us -> 145 us (0.70)
  Pallas kernels: 191 us -> 143 us
  local copies, waits for them, and re-layouts: 11 us -> 1.37 us
  other arithmetic: 2.94 us -> 0 us
    pallas_call x1 -> x2, Pallas kernels: 191 us -> 143 us  [the longest x1 139 us: shards(): pl.pallas_call(kernel, out_shape=shapes, in_specs=[hbm] * 5 + [vmem] * 8...]
    unnamed x4 -> x0, local copies, waits for them, and re-layouts: 4.62 us -> none
    add x6 -> x0, local copies, waits for them, and re-layouts: 3.27 us -> none  [the longest x2 1.58 us: shards(): lax.dynamic_index_in_dim(target * 32 + count, i, 0, False)[None, :]]
where the time goes in v2:
time: 145 us
  Pallas kernels  143 us (99%)
    pallas_call x1, Pallas kernels, shards(): pl.pallas_call(kernel, out_shape=shapes, in_specs=[hbm] * 5 + [vmem] * 8...  139 us
    pallas_call x1, Pallas kernels, shards(): pl.pallas_call(hand_over, grid=(4,), out_shape=shapes, in_specs=[tile, ti...  3.75 us

profile of v2, /device:TPU:1, one launch (start us, length us, event | category | flops | bytes accessed | tf_op | source)
XLA Modules:
  0.0 145.0 jit_solution(12640895761758465581)
XLA Ops:
  0.6 1.4 reshape.23.entries
  2.0 139.3 %shard_map.149 = (f32[256,1024]{1,0:T(8,128)}, f32[256,1024]{1,0:T(8,128)}) custom-call(f32[256,1024]{1,0:T(8,128)} %rc_hbm.1, f32[64,4096]{1,0:T(8,128)} %rp_hbm.1, bf16[4,1024,1024]{2,1,0:T(8,128)(2,1)} %bitcast.4, bf16[4,1024,1024]{2,1,0:T(8,128)(2,1)} %bitcast.5, bf16[32,8192]{1,0:T(8,128)(2,1)} %w_hbm.1, bf16[64,1024]{1,0:T(8,128)(2,1)} %uc.1, ...), custom_call_target="tpu_custom_call" | custom-call | tf_op jit(solution)/shard_map/pallas_call | solution.py:822
  141.3 3.8 %shard_map.150 = (f32[256,1024]{1,0:T(8,128)}, f32[256,1024]{1,0:T(8,128)}) custom-call(f32[256,1024]{1,0:T(8,128)} %get-tuple-element.4.xc, f32[256,1024]{1,0:T(8,128)} %get-tuple-element.5.xp), custom_call_target="tpu_custom_call" | custom-call | tf_op jit(solution)/shard_map/pallas_call | solution.py:849

commit v3 on v2

--- a/solution.py
+++ b/solution.py
@@ -80,7 +80,6 @@
     swap: Link
     sel_tall: Any
     sel_wide: Any
-    held: Any
     acc: Any
     bacc: Any
     rt: Any
@@ -122,7 +121,7 @@
         ysum=sums(SUBS, SUB, H),
         bsum=sums(1, NLOC // 2, 2 * RANK),
         z=Hops(pltpu.VMEM((COLS, SUBS, H, SUB), BF16), DMA((3, SUBS)), DMA((3, SUBS))),
-        kern=link((COLS, RANK, 2 * RANK), (2 * COLS, RANK, 2 * RANK), 2 * COLS),
+        kern=link((COLS,) + tile, (2 * COLS,) + tile, 2 * COLS),
         maps=link(None, (count // 2, 2) + tile, count // 2, F32),
     )
 
@@ -151,9 +150,8 @@
         swap=link(swap, swap, COLS),
         sel_tall=pltpu.VMEM((ROWS * 32, 512), BF16),
         sel_wide=pltpu.VMEM((512, ROWS * 32), BF16),
-        held=pltpu.VMEM((SUBS, SUB, H), F32),
         acc=pltpu.VMEM((SUBS, SUB, H), F32),
-        bacc=pltpu.VMEM((1, NLOC // 2, 2 * RANK), F32),
+        bacc=pltpu.VMEM((2, 1, NLOC // 2, 2 * RANK), F32),
         rt=pltpu.VMEM((NLOC, H), BF16),
         rpt=pltpu.VMEM((NLOC, H), F32),
         rpb=pltpu.VMEM((NLOC, H), BF16),
@@ -318,8 +316,7 @@
         ref = hops.buf.at[block] if whole else hops.buf.at[block, s]
         return remote(ref, ref, hops.sent.at[step, s], hops.came.at[step, s], i, to)
 
-    def v_start(f, vbase):
-        f.v.buf[c] = vbase[...]
+    def v_start(f):
         hop(f.v, 1, 0, True).start()
         hop(f.v, 0, 0, True).start()
 
@@ -402,6 +399,23 @@
 
         looped(0, sm.b.dst.shape[0], one)
 
+    def away(sm, piece, sent, ready=lambda n: None):
+        ready(0)
+        for p in range(SUBS // 2):
+            out = piece(diag, p).astype(BF16)
+            for k in range(2):
+                sm.a.src[2 * p + k] = out[k * SUB : (k + 1) * SUB]
+                within(sm, 2 * p + k).start()
+        ready(1)
+        for p in range(SUBS // 2):
+            out = piece(other, p)
+            for k in range(2):
+                s = 2 * p + k
+                within(sm, s).wait_recv()
+                sm.b.src[s] = (out[k * SUB : (k + 1) * SUB] + sm.a.dst[s].astype(F32)).astype(BF16)
+                if s < sent:
+                    between(sm, s).start()
+
     def b_send(sm, lo, hi):
         looped(lo, hi, lambda s: between(sm, s).start())
         if hi == sm.b.dst.shape[0]:
@@ -414,22 +428,24 @@
 
             pending.append(lambda: looped(0, subs, each))
 
+    def b_acc(f):
+        return m.bacc.at[0] if f is child else m.bacc.at[1]
+
     def b_sums(f):
-        piece = b_piece(f)
+        piece, acc = b_piece(f), b_acc(f)
         a_pieces(f.bsum, 0, diag, piece)
         a_send(f.bsum, 0)
         a_pieces(f.bsum, 1, peer, piece)
         a_send(f.bsum, 1)
-        own_pieces(f.bsum, m.bacc, other, piece)
-        b_make(f.bsum, m.bacc)
+        own_pieces(f.bsum, acc, other, piece)
+        b_make(f.bsum, acc)
         b_send(f.bsum, 0, 1)
-        own_pieces(f.bsum, m.bacc, c, piece)
-
-    def sum_wait(sm, s):
+        own_pieces(f.bsum, acc, c, piece)
+
+    def sum_wait(sm, s, acc):
         subs = sm.b.dst.shape[0]
         within(sm, subs + s).wait_recv()
         between(sm, s).wait_recv()
-        acc = m.bacc if subs == 1 else m.acc
         return acc[s] + sm.a.dst[subs + s].astype(F32) + sm.b.dst[s].astype(F32)
 
     def d_piece(f, rhs):
@@ -446,7 +462,7 @@
         return piece
 
     def b_finish(f):
-        packed = sum_wait(f.bsum, 0)
+        packed = sum_wait(f.bsum, 0, b_acc(f))
         out = jnp.concatenate([packed[:, :RANK], packed[:, RANK:]], axis=0)
         f.bl[...] = out.astype(BF16)
         high, low = high_low(out.T)
@@ -510,8 +526,10 @@
 
     def kernel_send(f, kernel_part, source):
         for k in range(COLS):
-            left = kernel_part if source is None else source[:, k * HS : (k + 1) * HS]
-            f.kern.src[k] = jnp.concatenate([left, kernel_part], axis=1).astype(BF16)
+            if source is None:
+                f.kern.src[k] = pack(kernel_part).astype(BF16)
+            else:
+                f.kern.src[k] = jnp.concatenate([source[:, k * HS : (k + 1) * HS], kernel_part], axis=1).astype(BF16)
         twin_send(f.kern)
 
     def route_values(rt, values):
@@ -559,74 +577,96 @@
         greet(i, lax.rem(c + d, COLS))
         greet(twin, lax.rem(c + d, COLS))
 
-    child.ut[...] = uc[...].astype(F32).T.astype(BF16)
-    parent.ut[...] = up[...].astype(F32).T.astype(BF16)
+    m.trans.dst[side] = jnp.concatenate([pc[...], pp[...]], axis=1)
+    child.v.buf[c] = vc[...]
+    parent.v.buf[c] = vp[...]
+    pl.semaphore_wait(barrier, ROWS - 1 + 2 * (COLS - 1))
+
+    v_start(child)
+    v_start(parent)
+    trans_copy = remote(
+        m.trans.dst.at[side], m.trans.dst.at[side], m.trans.sent.at[0], m.trans.came.at[0], twin, c
+    )
+    trans_from = remote(
+        m.trans.dst.at[1 - side], m.trans.dst.at[1 - side], m.trans.sent.at[0], m.trans.came.at[0], twin, c
+    )
+    trans_copy.start()
+    pending.append(trans_copy.wait_send)
     load_rc.wait()
     for s in range(SUBS):
         m.rt[s * SUB : (s + 1) * SUB, :] = m.rc[:, s * SUB : (s + 1) * SUB].T.astype(BF16)
+    child.ut[...] = uc[...].astype(F32).T.astype(BF16)
     y_part = d_piece(child, m.rt)
-    load(child, dc_hbm, 0).wait()
-    a_pieces(child.ysum, 0, diag, y_part)
-    load(child, dc_hbm, 1).wait()
-    own_pieces(child.ysum, m.held, other, y_part)
-    m.trans.dst[side] = jnp.concatenate([pc[...], pp[...]], axis=1)
-    pl.semaphore_wait(barrier, ROWS - 1 + 2 * (COLS - 1))
-
-    v_start(child, vc)
-    v_start(parent, vp)
-    trans_copy = remote(
-        m.trans.dst.at[side], m.trans.dst.at[side], m.trans.sent.at[0], m.trans.came.at[0], twin, c
-    )
-    trans_from = remote(
-        m.trans.dst.at[1 - side], m.trans.dst.at[1 - side], m.trans.sent.at[0], m.trans.came.at[0], twin, c
-    )
-    trans_copy.start()
-    pending.append(trans_copy.wait_send)
-    a_send(child.ysum, 0)
+    away(child.ysum, y_part, 0, lambda n: load(child, dc_hbm, n).wait())
+    eye = (
+        lax.broadcasted_iota(jnp.int32, (RANK, RANK), 0) == lax.broadcasted_iota(jnp.int32, (RANK, RANK), 1)
+    )
+    eye_f = eye.astype(F32)
+    left = lax.broadcasted_iota(jnp.int32, (RANK, 2 * RANK), 1) < RANK
+
+    def iota(rows, cols, axis):
+        return lax.broadcasted_iota(jnp.int32, (rows, cols), axis)
+
+    def over_lanes(mask, values):
+        return jnp.sum(jnp.where(mask, values, 0), axis=1, keepdims=True)
+
+    def over_rows(mask, values):
+        return jnp.sum(jnp.where(mask, values, 0), axis=0, keepdims=True)
+
+    wide = iota(RANK, 512, 1)
+    tall = iota(512, RANK, 0)
+
+    listed = jnp.concatenate([entries[:, :RANK], entries[:, RANK:]], axis=0)
+    held_here = ((listed >> 5) == i).astype(BF16)
+    below = (iota(RANK, RANK, 0) < iota(RANK, RANK, 1)).astype(BF16)
+    place = iota(ROWS, RANK, 0)
+    code = dot(held_here, below).astype(jnp.int32) + 32 * (2 * (place & (HALF - 1)) + (place >> 4))
+    wanted = i * 32 + (iota(RANK, RANK, 0) >> 1)
+    second_half = iota(RANK, RANK, 0) & 1
+    found = jnp.zeros((RANK, RANK), jnp.int32)
+    for j in range(ROWS):
+        hit = (listed[j : j + 1, :] == wanted) & (second_half == (2 * (j % HALF) + j // HALF) // HALF)
+        found = found + jnp.where(hit, code[j : j + 1, :], 0)
+    src_col = jnp.sum(found, axis=1, keepdims=True)
+    src_row = over_rows(eye, src_col)
+    src_tall = over_lanes(iota(512, RANK, 1) == (tall >> 3), src_row) + 4 * (iota(512, 1, 0) & 7)
+    src_wide = over_rows(iota(RANK, 512, 0) == (wide >> 3), src_col) + 4 * (iota(1, 512, 1) & 7)
+    m.sel_wide[...] = onehot((512, ROWS * 32), 1, src_tall)
+
     load(child, dc_hbm, 2).wait()
     load(child, dc_hbm, 3).wait()
     make_e(child)
     kernel_send(child, project(child.ehl, child.ut[...]), project(child.ehl, m.rt[...]))
+    load_rp.wait()
+    for k in range(COLS):
+        m.swap.src[k] = m.rp[:, k * NLOC : (k + 1) * NLOC].astype(BF16)
+    m.swap.dst[c] = m.swap.src[c]
+    col_send(m.swap)
+    b_send(child.ysum, 0, 1)
     a_pieces(child.ysum, 1, peer, y_part)
     a_send(child.ysum, 1)
     own_pieces(child.ysum, m.acc, c, y_part)
-    b_make(child.ysum, m.held)
+    parent.ut[...] = up[...].astype(F32).T.astype(BF16)
     trans_from.wait_recv()
     here = pair_place(child.maps)[2]
     for k, total in enumerate(twin_wait(child.kern)):
         transfer = m.trans.dst[k, :, :RANK] - total[:, RANK:]
         child.maps.dst[here, k] = jnp.concatenate([transfer, total[:, :RANK]], axis=1)
     pair_send(child.maps)
-    b_send(child.ysum, 0, SUBS - 1)
     for n in range(COLS):
         load(parent, dp_hbm, n).wait()
     make_e(parent)
     kernel_send(parent, project(parent.ehl, parent.ut[...]), None)
-    b_send(child.ysum, SUBS - 1, SUBS)
+    b_send(child.ysum, 1, SUBS)
     b_sums(child)
 
-    eye = (
-        lax.broadcasted_iota(jnp.int32, (RANK, RANK), 0) == lax.broadcasted_iota(jnp.int32, (RANK, RANK), 1)
-    )
-    eye_f = eye.astype(F32)
-    left = lax.broadcasted_iota(jnp.int32, (RANK, 2 * RANK), 1) < RANK
-
-    def iota(rows, cols, axis):
-        return lax.broadcasted_iota(jnp.int32, (rows, cols), axis)
-
-    def over_lanes(mask, values):
-        return jnp.sum(jnp.where(mask, values, 0), axis=1, keepdims=True)
-
-    def over_rows(mask, values):
-        return jnp.sum(jnp.where(mask, values, 0), axis=0, keepdims=True)
-
-    mine = entries[pl.ds(i, 1), :] >> 5
+    pairs = entries[pl.ds(lax.div(i, 2), 1), :] >> 5
+    mine = jnp.where(side == 0, pairs[:, :RANK], pairs[:, RANK:])
     mine_col = over_lanes(eye, mine)
     earlier = (mine_col == mine) & (iota(RANK, RANK, 1) < iota(RANK, RANK, 0))
     tgt_col = mine_col * 32 + jnp.sum(earlier.astype(jnp.int32), axis=1, keepdims=True)
     tgt_row = over_rows(eye, tgt_col)
-    wide = iota(RANK, 512, 1)
-    tall = iota(512, RANK, 0)
+    tgt_tall = over_lanes(iota(512, RANK, 1) == (tall & (RANK - 1)), tgt_row) + 4 * (iota(512, 1, 0) >> 6)
     by_group = over_rows(iota(RANK, 512, 0) == (wide & (RANK - 1)), tgt_col) + 4 * (iota(1, 512, 1) >> 6)
     by_block = over_rows(iota(RANK, 512, 0) == (wide >> 3), tgt_col) + 4 * (iota(1, 512, 1) & 7)
     m.sel_tall[...] = onehot((ROWS * 32, 512), 0, by_block)
@@ -641,12 +681,7 @@
         allowed = iota(RANK, BLK, 0) < ranks[g]
         m.msk[:, cols] = jnp.where(allowed, wf[:, cols].astype(F32), 0.0).astype(BF16)
 
-    here = pair_place(parent.maps)[2]
-    for k, total in enumerate(twin_wait(parent.kern)):
-        parent.maps.dst[here, k] = pack(m.trans.dst[k, :, RANK:] - total[:, RANK:])
-    pair_send(parent.maps)
     pair_wait(child.maps)
-    row_send(weights.rows)
 
     def store_phi(sc, j, value):
         sc.phi[pl.ds(pl.multiple_of(j * (RANK // 2), RANK // 2), RANK // 2), :] = pack(value)
@@ -660,15 +695,21 @@
         return jnp.where(moves, product + added, both)
 
     both = lax.fori_loop(
-        0, HALF, child_step, jnp.concatenate([jnp.zeros((RANK, RANK), F32), eye_f], axis=1)
+        0, HALF, child_step, jnp.concatenate([jnp.zeros((RANK, RANK), F32), eye_f], axis=1), unroll=4
     )
     send_state(m.first, both[:, :RANK])
+    here = pair_place(parent.maps)[2]
+    for k, total in enumerate(twin_wait(parent.kern)):
+        parent.maps.dst[here, k] = pack(m.trans.dst[k, :, RANK:]) - total
+    pair_send(parent.maps)
+    row_send(weights.rows)
+    b_sums(parent)
     b_finish(child)
     h_child = wait_state(m.first)
 
     def child_y(s):
         rows = pl.ds(pl.multiple_of(s * SUB, SUB), SUB)
-        value = sum_wait(child.ysum, s) - dot(child.bl[rows, :], h_child)
+        value = sum_wait(child.ysum, s, m.acc) - dot(child.bl[rows, :], h_child)
         m.y[rows, :] = value
         m.yb[rows, :] = value.astype(BF16)
 
@@ -679,45 +720,32 @@
         ).astype(BF16)
     route_rows(factors, dot(m.sel_tall[...], m.fac[...]))
 
-    load_rp.wait()
-    for k in range(COLS):
-        m.swap.src[k] = m.rp[:, k * NLOC : (k + 1) * NLOC].astype(BF16)
-    m.swap.dst[c] = m.swap.src[c]
-    col_send(m.swap)
-    b_sums(parent)
-
-    held_here = ((entries[...] >> 5) == i).astype(BF16)
-    below = (iota(RANK, RANK, 0) < iota(RANK, RANK, 1)).astype(BF16)
-    code = dot(held_here, below).astype(jnp.int32) + 32 * iota(ROWS, RANK, 0)
-    wanted = i * 32 + (iota(RANK, RANK, 0) >> 1)
-    second_half = iota(RANK, RANK, 0) & 1
-    found = jnp.zeros((RANK, RANK), jnp.int32)
-    for j in range(ROWS):
-        hit = (entries[j : j + 1, :] == wanted) & (second_half == j // HALF)
-        found = found + jnp.where(hit, code[j : j + 1, :], 0)
-    src_col = jnp.sum(found, axis=1, keepdims=True)
-    src_row = over_rows(eye, src_col)
-    src_tall = over_lanes(iota(512, RANK, 1) == (tall >> 3), src_row) + 4 * (iota(512, 1, 0) & 7)
-    src_wide = over_rows(iota(RANK, 512, 0) == (wide >> 3), src_col) + 4 * (iota(1, 512, 1) & 7)
-    tgt_tall = over_lanes(iota(512, RANK, 1) == (tall & (RANK - 1)), tgt_row) + 4 * (iota(512, 1, 0) >> 6)
-    m.sel_wide[...] = onehot((512, ROWS * 32), 1, src_tall)
     weights.cols.src[...] = dot(m.sel_wide[...], rows_of(weights)).astype(BF16).reshape(COLS, 128, BLK)
     route_cols(weights)
     pair_wait(parent.maps)
 
-    def parent_step(n, pair):
-        rising, falling = pair
-        j = ROWS - 1 - n
-        store_phi(back, n, jnp.where(n > i, rising, 0.0))
-        store_phi(ahead, j, jnp.where(j < i, falling, 0.0).T)
-        up_next = jnp.dot(unpack(parent.maps.dst[lax.div(n, 2), lax.rem(n, 2)]), rising, precision=HIGH)
-        down_next = jnp.dot(falling, unpack(parent.maps.dst[lax.div(j, 2), lax.rem(j, 2)]), precision=HIGH)
-        return jnp.where(n > i, up_next, rising), jnp.where(j < i, down_next, falling)
-
-    lax.fori_loop(0, ROWS, parent_step, (eye_f, eye_f))
+    def map_of(j):
+        return unpack(parent.maps.dst[lax.div(j, 2), lax.rem(j, 2)])
+
+    def falling_step(n, pair):
+        out = []
+        for start, now in ((ROWS, pair[0]), (HALF, pair[1])):
+            j = start - 1 - n
+            store_phi(ahead, j, jnp.where(j < i, now, 0.0).T)
+            out.append(jnp.where(j < i, jnp.dot(now, map_of(j), precision=HIGH), now))
+        return tuple(out)
+
+    def rising_step(n, now):
+        store_phi(back, n, jnp.where(n > i, now, 0.0))
+        return jnp.where(n > i, jnp.dot(map_of(n), now, precision=HIGH), now)
+
+    upper, _ = lax.fori_loop(0, HALF, falling_step, (eye_f, eye_f), unroll=4)
+    for k in range(2):
+        part = (slice(0, HALF * RANK // 2), slice(k * RANK, (k + 1) * RANK))
+        ahead.phi[part] = lax.dot_general(
+            ahead.phi[part], upper, (((1,), (1,)), ((), ())), precision=HIGH, preferred_element_type=F32
+        )
     split_phi(ahead)
-    split_phi(back)
-    split_phi(child_back)
     col_wait(m.swap)
     for k in range(SUBS):
         cols = slice(k * SUB, (k + 1) * SUB)
@@ -742,22 +770,21 @@
 
     scan_one(ahead, project(parent.ehl, m.rpb[...]))
     y_part = d_piece(parent, m.rpb)
-    a_pieces(parent.ysum, 0, diag, y_part)
-    a_send(parent.ysum, 0)
-    own_pieces(parent.ysum, m.held, other, y_part)
-    b_make(parent.ysum, m.held)
-    b_send(parent.ysum, 0, SUBS - 1)
+    away(parent.ysum, y_part, SUBS - 1)
     scan_two(ahead)
     a_pieces(parent.ysum, 1, peer, y_part)
     a_send(parent.ysum, 1)
     own_pieces(parent.ysum, m.acc, c, y_part)
     scan_three(ahead)
     b_send(parent.ysum, SUBS - 1, SUBS)
+    lax.fori_loop(0, ROWS, rising_step, eye_f, unroll=4)
+    split_phi(back)
+    split_phi(child_back)
     h_parent = wait_state(ahead.state)
 
     def parent_y(s):
         rows = pl.ds(pl.multiple_of(s * SUB, SUB), SUB)
-        m.rpb[rows, :] = (sum_wait(parent.ysum, s) - dot(parent.bl[rows, :], h_parent)).astype(BF16)
+        m.rpb[rows, :] = (sum_wait(parent.ysum, s, m.acc) - dot(parent.bl[rows, :], h_parent)).astype(BF16)
 
     looped(0, SUBS, parent_y)
     scan_one(back, project(parent.fhl, m.rpb[...]))
@@ -806,9 +833,24 @@
         done()
 
 
-def hand_over(xc, xp, xc_out, xp_out):
-    xc_out[...] = xc[...]
-    xp_out[...] = xp[...]
+def hand_over(xc, xp, xc_out, xp_out, buf, arrive, leave):
+    steps = []
+    for k, (src, dst) in enumerate(((xc, xc_out), (xp, xp_out))):
+        for q in range(SUBS):
+            rows = pl.ds(q * HS, HS)
+            steps.append(
+                (
+                    pltpu.make_async_copy(src.at[rows, :], buf.at[k, rows, :], arrive.at[k, q]),
+                    pltpu.make_async_copy(buf.at[k, rows, :], dst.at[rows, :], leave.at[k, q]),
+                )
+            )
+    for come, _ in steps:
+        come.start()
+    for come, go in steps:
+        come.wait()
+        go.start()
+    for _, go in steps:
+        go.wait()
 
 
 def shards(
@@ -841,17 +883,16 @@
         w_first,
         trans_child.reshape(RANK, RANK),
         trans_parent.reshape(RANK, RANK),
-        extend_map.reshape(ROWS, RANK),
+        extend_map.reshape(HALF, 2 * RANK),
         block_ranks,
     )
-    tile = pl.BlockSpec((H // 4, NLOC), lambda n: (n, 0))
     return tuple(
         pl.pallas_call(
             hand_over,
-            grid=(4,),
             out_shape=shapes,
-            in_specs=[tile, tile],
-            out_specs=[tile, tile],
+            in_specs=[hbm, hbm],
+            out_specs=[hbm, hbm],
+            scratch_shapes=[pltpu.VMEM((2, H, NLOC), F32), DMA((2, SUBS)), DMA((2, SUBS))],
         )(x_child, x_parent)
     )
 

time: 145 us -> 138 us (0.952)
  Pallas kernels: 143 us -> 137 us
    pallas_call x1, Pallas kernels: 139 us -> 135 us  [shards(): pl.pallas_call(kernel, out_shape=shapes, in_specs=[hbm] * 5 + [vmem] * 8...]
where the time goes in v3:
time: 138 us
  Pallas kernels  137 us (99%)
    pallas_call x1, Pallas kernels, shards(): pl.pallas_call(kernel, out_shape=shapes, in_specs=[hbm] * 5 + [vmem] * 8...  135 us

profile of v3, /device:TPU:1, one launch (start us, length us, event | category | flops | bytes accessed | tf_op | source)
XLA Modules:
  0.0 137.9 jit_solution(13245639031081077302)
XLA Ops:
  0.6 134.6 %shard_map.149 = (f32[256,1024]{1,0:T(8,128)}, f32[256,1024]{1,0:T(8,128)}) custom-call(f32[256,1024]{1,0:T(8,128)} %rc_hbm.1, f32[64,4096]{1,0:T(8,128)} %rp_hbm.1, bf16[4,1024,1024]{2,1,0:T(8,128)(2,1)} %bitcast.5, bf16[4,1024,1024]{2,1,0:T(8,128)(2,1)} %bitcast.6, bf16[32,8192]{1,0:T(8,128)(2,1)} %w_hbm.1, bf16[64,1024]{1,0:T(8,128)(2,1)} %uc.1, ...), custom_call_target="tpu_custom_call" | custom-call | tf_op jit(solution)/shard_map/pallas_call | solution.py:864
  135.3 2.4 %shard_map.150 = (f32[256,1024]{1,0:T(8,128)}, f32[256,1024]{1,0:T(8,128)}) custom-call(f32[256,1024]{1,0:T(8,128)} %get-tuple-element.4.xc, f32[256,1024]{1,0:T(8,128)} %get-tuple-element.5.xp), custom_call_target="tpu_custom_call" | custom-call | tf_op jit(solution)/shard_map/pallas_call | solution.py:890

commit v4 on v3

--- a/solution.py
+++ b/solution.py
@@ -329,14 +329,13 @@
         def one(s):
             piece = source[pl.ds(pl.multiple_of(s * SUB, SUB), SUB), :]
             f.z.buf[c, s] = piece.astype(F32).T.astype(BF16)
-            hop(f.z, 0, s).start()
 
         def first(s):
             one(s)
             hop(f.z, 1, s).start()
-
-        looped(0, SUBS - 1, first)
-        one(SUBS - 1)
+            hop(f.z, 0, s).start()
+
+        looped(0, SUBS, first)
 
         def each(s):
             for step in range(3):
@@ -793,7 +792,6 @@
     scan_two(back)
     z_apply(parent, peer, m.xp, 0)
     scan_three(back)
-    hop(parent.z, 1, SUBS - 1).start()
     z_apply(parent, other, m.xp, 1)
     z_apply(parent, diag, m.xp, 2)
     g_parent = wait_state(back.state)
@@ -816,12 +814,15 @@
         m.yb[rows, :] = (m.y[rows, :] - correction).astype(BF16)
 
     scan_one(child_back, project(child.fhl, m.yb[...]))
+    sent_before = list(pending)
+    pending.clear()
     z_start(child, m.yb)
     z_apply(child, c, m.rc, None)
     scan_two(child_back)
+    for done in sent_before:
+        done()
     z_apply(child, peer, m.rc, 0)
     scan_three(child_back)
-    hop(child.z, 1, SUBS - 1).start()
     z_apply(child, other, m.rc, 1)
     z_apply(child, diag, m.rc, 2)
     g_child = wait_state(child_back.state)

time: 138 us -> 135 us (0.978)
  Pallas kernels: 137 us -> 135 us
    pallas_call x1, Pallas kernels: 135 us -> 132 us  [shards(): pl.pallas_call(kernel, out_shape=shapes, in_specs=[hbm] * 5 + [vmem] * 8...]
where the time goes in v4:
time: 135 us
  Pallas kernels  135 us (100%)
    pallas_call x1, Pallas kernels, shards(): pl.pallas_call(kernel, out_shape=shapes, in_specs=[hbm] * 5 + [vmem] * 8...  132 us

profile of v4, /device:TPU:1, one launch (start us, length us, event | category | flops | bytes accessed | tf_op | source)
XLA Modules:
  0.0 135.3 jit_solution(7514303264302122133)
XLA Ops:
  0.6 132.1 %shard_map.149 = (f32[256,1024]{1,0:T(8,128)}, f32[256,1024]{1,0:T(8,128)}) custom-call(f32[256,1024]{1,0:T(8,128)} %rc_hbm.1, f32[64,4096]{1,0:T(8,128)} %rp_hbm.1, bf16[4,1024,1024]{2,1,0:T(8,128)(2,1)} %bitcast.5, bf16[4,1024,1024]{2,1,0:T(8,128)(2,1)} %bitcast.6, bf16[32,8192]{1,0:T(8,128)(2,1)} %w_hbm.1, bf16[64,1024]{1,0:T(8,128)(2,1)} %uc.1, ...), custom_call_target="tpu_custom_call" | custom-call | tf_op jit(solution)/shard_map/pallas_call | solution.py:865
  132.8 2.4 %shard_map.150 = (f32[256,1024]{1,0:T(8,128)}, f32[256,1024]{1,0:T(8,128)}) custom-call(f32[256,1024]{1,0:T(8,128)} %get-tuple-element.4.xc, f32[256,1024]{1,0:T(8,128)} %get-tuple-element.5.xp), custom_call_target="tpu_custom_call" | custom-call | tf_op jit(solution)/shard_map/pallas_call | solution.py:891
